TPU v7x, 256 devices: a whole 4x4x8 slice. The times are simulated.
256 devices in a mesh: dp: 16 (over y, x), feat: 16 (over z, core).
Axes of the slice: x: 4, y: 4, z: 8, core: 2. Of those that a mesh axis runs over, the one named last changes fastest.
Arguments:
- features: bfloat16 [262144, 768], P('dp', 'feat'), may hold values from -6 to 6
- target_ids: int32 [131072], P('dp'), may hold values from 0 to 16383
- tile_index: int32 [1024, 4], P('dp'), may hold values from 0 to 127
- tile_count: int32 [1024], P('dp'), may hold values from 1 to 4, as said below
- tile_values: bfloat16 [1024, 4, 128, 128], P('dp'), may hold values from 0 to 0.088378906
- w_neigh: bfloat16 [768, 1024], P('feat'), may hold values from -0.21875 to 0.21875
- w_self: bfloat16 [768, 1024], P('feat'), may hold values from -0.21875 to 0.21875
- bias: float32 [1024], replicated, may hold values from -3 to 3
- cotangent: bfloat16 [131072, 1024], P(('dp', 'feat')), may hold values from -0.125 to 0.125
Outputs:
- activation: bfloat16 [131072, 1024], P(('dp', 'feat'))
- grad_neigh: float32 [768, 1024], P('feat', 'dp')
- grad_self: float32 [768, 1024], P('feat', 'dp')
Inputs may be any that keep to these rules, and one draw needn't show every extreme that they name: `tile_count`: in every replica some target block has all 4 slots live. `tile_index`: source blocks may repeat within a target block. `target_ids`: target rows may repeat.
All inputs are finite; a program needn't handle non-finite values.
Results may differ from a plain program's by a relative error of at most 0.0053.
Values may be sent and summed in bfloat16 or wider, within the bound.
No kernel may reach another device: no remote copies, remote signals or barrier semaphores. Data moves between devices by JAX's collectives and lax.ppermute only.
A program may use at most 128 MiB of HBM per device.

v0:
```python
import functools

import jax
import jax.numpy as jnp
import numpy as np
from jax import lax
from jax.experimental import pallas as pl
from jax.experimental.pallas import tpu as pltpu
from jax.sharding import Mesh, PartitionSpec as P

TILE = 128
COLS = 48
NZ, NC, NY, NX = 8, 2, 4, 4
CHIP = 1024
HALF = 512
PIECE = 32
GATE = 0.7978845608028654
CUBE = 0.044715
BF, F32 = jnp.bfloat16, jnp.float32
VMEM = pl.BlockSpec(memory_space=pltpu.VMEM)
SMEM = pl.BlockSpec(memory_space=pltpu.SMEM)
ANY = pl.BlockSpec(memory_space=pl.ANY)
HBM = pl.BlockSpec(memory_space=pltpu.HBM)


def params(mib=56):
    return pltpu.CompilerParams(vmem_limit_bytes=mib * 2**20)


def nt(left, right):
    return lax.dot_general(left, right, (((1,), (1,)), ((), ())), preferred_element_type=F32)


WIDE = 256
PER = 4


def aggregate_kernel(half, index_ref, count_ref, feat_hbm, tiles_hbm, *rest):
    out_ref, feat, tiles, sems = rest[-4:]

    def tile_copy(z):
        src = tiles_hbm.at[pl.ds(z * 2 * PER + half * PER, PER)]
        return pltpu.make_async_copy(src, tiles.at[pl.ds(z * PER, PER)], sems.at[z])

    feat_copy = pltpu.make_async_copy(feat_hbm, feat, sems.at[NZ])
    feat_copy.start()
    for z in range(NZ):
        tile_copy(z).start()
    if half == 0:
        neigh_ref, self_ref = rest[:2]
        x, y = lax.axis_index("x"), lax.axis_index("y")
        weights = [neigh_ref[:, pl.ds(pl.multiple_of(y * WIDE, WIDE), WIDE)]]
        for far in range(NY):
            lanes = pl.ds(pl.multiple_of(far * WIDE + (x // 2) * TILE, TILE), TILE)
            both = self_ref[:, lanes].astype(F32)
            weights.append(jnp.where(lax.rem(x, 2) == 1, both[:, 64:], both[:, :64]).astype(BF))
        weights = jnp.concatenate(weights, axis=1)
        for z in range(NZ):
            out_ref[z, :, HALF:] = weights
    feat_copy.wait()

    def chip(z, _):
        tile_copy(z).wait()
        for blk in range(PER):
            at = z * 2 * PER + half * PER + blk
            live = count_ref[at]
            sources, held = [], []
            for slot in range(4):
                start = pl.multiple_of(index_ref[slot, at] * TILE, TILE)
                part = feat[:, pl.ds(start, TILE)]
                sources.append(jnp.where(slot < live, part, jnp.zeros_like(part)))
                held.append(tiles[z * PER + blk, slot])
            total = nt(jnp.concatenate(sources, axis=1), jnp.concatenate(held, axis=1))
            out_ref[z, :, blk * TILE : (blk + 1) * TILE] = total.astype(BF)
        return 0

    lax.fori_loop(0, NZ, chip, 0)


def aggregate(half, feat_t, index, count, tiles, extra):
    width = CHIP if half == 0 else HALF
    return pl.pallas_call(
        functools.partial(aggregate_kernel, half),
        in_specs=[SMEM, SMEM, ANY, ANY] + ([VMEM, VMEM] if half == 0 else [ANY]),
        out_specs=VMEM,
        out_shape=jax.ShapeDtypeStruct((NZ, COLS, width), BF),
        scratch_shapes=[
            pltpu.VMEM(feat_t.shape, BF),
            pltpu.VMEM((NZ * PER, *tiles.shape[1:]), BF),
            pltpu.SemaphoreType.DMA((NZ + 1,)),
        ],
        compiler_params=params(56),
        cost_estimate=pl.CostEstimate(flops=200_000_000, bytes_accessed=6_000_000, transcendentals=0),
        name="aggregate",
    )(index, count, feat_t, tiles, *extra)


def pick_kernel(core_ref, mine_ref, other_ref, neigh_ref, self_ref):
    width = NZ * COLS
    first = core_ref[0] == 0
    for part, out in enumerate((neigh_ref, self_ref)):
        lanes = slice(part * WIDE, (part + 1) * WIDE)
        turned = [ref[:, :, lanes].reshape(width, WIDE).astype(F32).T for ref in (mine_ref, other_ref)]
        for i in range(4):
            cut = [v[i * 64 : (i + 1) * 64] for v in turned]
            mine, other = [jnp.where(first, v[:PIECE], v[PIECE:]) for v in cut]
            out[i, :, :width] = jnp.where(first, mine, other).astype(BF)
            out[i, :, width:] = jnp.where(first, other, mine).astype(BF)


def pick_weights(core, mine, other):
    tail = pl.BlockSpec((NZ, COLS, 2 * WIDE), lambda i: (0, 0, 1))
    shape = (4, PIECE, NC * NZ * COLS)
    return pl.pallas_call(
        pick_kernel,
        grid=(1,),
        in_specs=[SMEM, tail, tail],
        out_specs=[pl.BlockSpec(shape, lambda i: (0, 0, 0))] * 2,
        out_shape=[jax.ShapeDtypeStruct(shape, BF)] * 2,
        compiler_params=params(16),
        cost_estimate=pl.CostEstimate(flops=0, bytes_accessed=1_600_000, transcendentals=0),
        name="pick_weights",
    )(core, mine, other)


GROUP = 128


def own_kernel(ids_ref, feat_ref, agg_ref, out_ref, rows, picked):
    out_ref[:, :, CHIP:] = agg_ref[...]
    wide = 512

    def spread(i, _):
        at = pl.multiple_of(i * wide, wide)
        rows[pl.ds(at, wide), 0:COLS] = feat_ref[:, pl.ds(at, wide)].astype(F32).T
        return 0

    lax.fori_loop(0, feat_ref.shape[1] // wide, spread, 0)

    def block(z, _):
        def group(g, _):
            base = g * GROUP
            for j in range(GROUP):
                picked[pl.ds(base + j, 1), :] = rows[pl.ds(ids_ref[z * CHIP + base + j], 1), :]
            return 0

        lax.fori_loop(0, CHIP // GROUP, group, 0)
        out_ref[z, :, :CHIP] = picked[:, 0:COLS].T.astype(BF)
        return 0

    lax.fori_loop(0, NZ, block, 0)


def own(feat_t, ids, agg):
    return pl.pallas_call(
        own_kernel,
        in_specs=[SMEM, VMEM, VMEM],
        out_specs=VMEM,
        out_shape=jax.ShapeDtypeStruct((NZ, COLS, CHIP + HALF), BF),
        scratch_shapes=[pltpu.VMEM((feat_t.shape[1], TILE), F32), pltpu.VMEM((CHIP, TILE), F32)],
        compiler_params=params(20),
        cost_estimate=pl.CostEstimate(flops=0, bytes_accessed=60_000_000, transcendentals=0),
        name="own_rows",
    )(ids, feat_t, agg)


def turn_kernel(core_ref, cot_ref, after_ref, mine_ref, other_ref):
    turned = cot_ref[...].astype(F32).T.astype(BF)
    low = jnp.concatenate([turned[0:32], turned[64:96]], axis=0)
    high = jnp.concatenate([turned[32:64], turned[96:128]], axis=0)
    first = core_ref[0] == 0
    mine_ref[...] = jnp.where(first, low, high)
    other_ref[...] = jnp.where(first, high, low)


def turn(core, cot, after):
    half = jax.ShapeDtypeStruct((HALF, HALF), BF)
    return pl.pallas_call(
        turn_kernel,
        grid=(8,),
        in_specs=[SMEM, pl.BlockSpec((HALF, TILE), lambda i: (0, i))] + [ANY],
        out_specs=[pl.BlockSpec((64, HALF), lambda i: (i, 0))] * 2,
        out_shape=[half, half],
        compiler_params=params(12),
        cost_estimate=pl.CostEstimate(flops=0, bytes_accessed=4_000_000, transcendentals=0),
        name="turn_cotangent",
    )(core, cot, after)


def unturn_kernel(core_ref, mine_ref, other_ref, out_ref, token_ref):
    first = core_ref[0] == 0
    low = jnp.where(first, mine_ref[...], other_ref[...])
    high = jnp.where(first, other_ref[...], mine_ref[...])
    both = jnp.concatenate([low[0:32], high[0:32], low[32:64], high[32:64]], axis=0)
    out_ref[...] = both.astype(F32).T.astype(BF)
    token_ref[...] = jnp.zeros_like(token_ref)


def unturn(core, mine, other):
    return pl.pallas_call(
        unturn_kernel,
        grid=(8,),
        in_specs=[SMEM] + [pl.BlockSpec((64, HALF), lambda i: (i, 0))] * 2,
        out_specs=[pl.BlockSpec((HALF, TILE), lambda i: (0, i)), pl.BlockSpec((8, TILE), lambda i: (0, 0))],
        out_shape=[jax.ShapeDtypeStruct((HALF, 1024), BF), jax.ShapeDtypeStruct((8, TILE), F32)],
        compiler_params=params(12),
        cost_estimate=pl.CostEstimate(flops=0, bytes_accessed=4_000_000, transcendentals=0),
        name="unturn_activation",
    )(core, mine, other)


def hand_kernel(*refs):
    pass


def hand_on(value, after):
    return pl.pallas_call(
        hand_kernel,
        in_specs=[HBM] * (1 + len(after)),
        out_specs=HBM,
        out_shape=jax.ShapeDtypeStruct(value.shape, value.dtype),
        input_output_aliases={0: 0},
        compiler_params=params(16),
        cost_estimate=pl.CostEstimate(flops=0, bytes_accessed=0, transcendentals=0),
        name="hand_on",
    )(value, *after)


def layer_kernel(
    place_ref, agg_mine, agg_other, own_mine, own_other, n0, n1, n2, n3, s0, s1, s2, s3, bias_ref,
    cot_mine, cot_other, act_mine, act_other, grad_hbm, nodes, weights, cot, act, grads, in_sems, out_sems,
):
    core, x, y = place_ref[0], place_ref[1], place_ref[2]
    here = pl.ds(pl.multiple_of(core * HALF, HALF), HALF)
    there = pl.ds(pl.multiple_of((1 - core) * HALF, HALF), HALF)
    pairs = []
    for first, second, at in ((agg_mine, own_mine, core), (agg_other, own_other, 1 - core)):
        pairs.append((first.at[:, :, pl.ds(0, HALF)], nodes.at[at, :, :, pl.ds(0, HALF)]))
        pairs.append((second.at[:, :, pl.ds(CHIP, HALF)], nodes.at[at, :, :, pl.ds(HALF, HALF)]))
        pairs.append((second.at[:, :, pl.ds(0, CHIP)], nodes.at[2 + at]))
    for far, (over_y, over_x) in enumerate(zip((n0, n1, n2, n3), (s0, s1, s2, s3))):
        for near in range(4):
            from_y, from_x = lax.rem(y - far + NY, NY) * NX + near, near * NX + lax.rem(x - far + NX, NX)
            for half, ref, block in ((0, over_y, from_y), (1, over_x, from_x)):
                pairs.append((ref.at[near], weights.at[block, :, pl.ds(half * 768, 768)]))
    pairs += [
        (cot_mine, cot.at[:, here]),
        (cot_other, cot.at[:, there]),
    ]
    copies = [pltpu.make_async_copy(src, dst, in_sems.at[i]) for i, (src, dst) in enumerate(pairs)]
    for copy in copies:
        copy.start()
    for copy in copies:
        copy.wait()
    held = nodes[...].reshape(1536, CHIP)
    rows = HALF // 2
    sent = []

    def send(src, dst):
        sent.append(pltpu.make_async_copy(src, dst, out_sems.at[len(sent)]))
        sent[-1].start()

    for chunk in range(2):
        at = pl.ds(chunk * rows, rows)
        own_weights = weights[chunk * 8 : (chunk + 1) * 8].reshape(rows, 1536)
        v = jnp.dot(own_weights, held, preferred_element_type=F32) + bias_ref[at, :]
        sq = v * v
        t = jnp.tanh(GATE * (v + CUBE * (sq * v)))
        half = 0.5 * (1.0 + t)
        act[at, :] = (v * half).astype(BF)
        send(act.at[at, here], act_mine.at[at])
        send(act.at[at, there], act_other.at[at])
        slope = half + (0.5 * GATE) * v * (1.0 - t * t) * (1.0 + (3.0 * CUBE) * sq)
        grad = (cot[at, :].astype(F32) * slope).astype(BF)
        grads[chunk * 8 : (chunk + 1) * 8] = nt(grad, held).astype(BF).reshape(8, PIECE, 1536)
        for part in range(2):
            for side in range(NC):
                src = grads.at[pl.ds(chunk * 8, 8), :, pl.ds((part * NC + side) * 384, 384)]
                send(src, grad_hbm.at[pl.ds(chunk * 8, 8), side, :, pl.ds(part * 384, 384)])
    for copy in sent:
        copy.wait()


def layer(place, aggs, owns, weights, bias, cots):
    half = jax.ShapeDtypeStruct((HALF, HALF), BF)
    return pl.pallas_call(
        layer_kernel,
        in_specs=[SMEM] + [HBM] * 12 + [VMEM] + [HBM] * 2,
        out_specs=[HBM] * 3,
        out_shape=[half, half, jax.ShapeDtypeStruct((16, NC, PIECE, 768), BF)],
        scratch_shapes=[
            pltpu.VMEM((4, NZ, COLS, CHIP), BF),
            pltpu.VMEM((16, PIECE, 1536), BF),
            pltpu.VMEM((HALF, CHIP), BF),
            pltpu.VMEM((HALF, CHIP), BF),
            pltpu.VMEM((16, PIECE, 1536), BF),
            pltpu.SemaphoreType.DMA((40,)),
            pltpu.SemaphoreType.DMA((12,)),
        ],
        compiler_params=params(56),
        cost_estimate=pl.CostEstimate(flops=3_200_000_000, bytes_accessed=9_000_000, transcendentals=524288),
        name="layer",
    )(place, *aggs, *owns, *weights, bias, *cots)


def add_kernel(in_hbm, token_ref, out_ref, held, sems):
    copies = [pltpu.make_async_copy(in_hbm.at[i], held.at[i], sems.at[i]) for i in range(32)]
    for copy in copies:
        copy.start()
    totals = [None, None]
    for i, copy in enumerate(copies):
        copy.wait()
        term = held[i].astype(F32)
        totals[i % 2] = term if totals[i % 2] is None else totals[i % 2] + term
    total = jnp.concatenate(totals, axis=0)
    for z in range(NZ):
        cut = [total[:, (part * NZ + z) * COLS :][:, :COLS] for part in range(2)]
        out_ref[z] = jnp.concatenate(cut, axis=1).astype(BF)


def add_pieces(pieces, token):
    return pl.pallas_call(
        add_kernel,
        in_specs=[ANY, ANY],
        out_specs=VMEM,
        out_shape=jax.ShapeDtypeStruct((NZ, 64, 2 * COLS), BF),
        scratch_shapes=[pltpu.VMEM((32, PIECE, 768), BF), pltpu.SemaphoreType.DMA((32,))],
        compiler_params=params(8),
        cost_estimate=pl.CostEstimate(flops=800_000, bytes_accessed=1_700_000, transcendentals=0),
        name="add_pieces",
    )(pieces, token)


def last_kernel(in_ref, neigh_ref, self_ref):
    total = in_ref[0].astype(F32)
    for z in range(1, NZ):
        total = total + in_ref[z].astype(F32)
    turned = total.T
    neigh_ref[...] = turned[:COLS]
    self_ref[...] = turned[COLS:]


def add_last(pieces):
    shape = jax.ShapeDtypeStruct((COLS, 64), F32)
    return pl.pallas_call(
        last_kernel,
        in_specs=[VMEM],
        out_specs=[VMEM, VMEM],
        out_shape=[shape, shape],
        compiler_params=params(8),
        cost_estimate=pl.CostEstimate(flops=50_000, bytes_accessed=200_000, transcendentals=0),
        name="add_last",
    )(pieces)


def swap(value):
    return lax.ppermute(value, "core", [(0, 1), (1, 0)])


def spread_ring(value, axis, size):
    return [value] + [
        lax.ppermute(value, axis, [(i, (i + s) % size) for i in range(size)]) for s in range(1, size)
    ]


def shards(features, target_ids, tile_index, tile_count, tile_values, w_neigh, w_self, bias, cotangent):
    core, x, y = lax.axis_index("core"), lax.axis_index("x"), lax.axis_index("y")
    core_at = core.astype(jnp.int32).reshape(1)
    place = jnp.stack([core, x, y]).astype(jnp.int32)
    feat_t = features.T

    bias_here = lax.dynamic_index_in_dim(bias.reshape(16, NC, PIECE), core, 1, keepdims=False).reshape(HALF, 1)

    agg_sent = aggregate(0, feat_t, tile_index.T, tile_count, tile_values, (w_neigh, w_self))
    agg = lax.all_to_all(agg_sent, "z", 0, 0)
    agg_late = aggregate(1, feat_t, tile_index.T, tile_count, tile_values, (agg_sent,))
    own_sent = own(feat_t, target_ids, agg_late)
    own_rows = lax.all_to_all(own_sent, "z", 0, 0)

    agg = hand_on(agg, (own_sent,))
    agg_swapped = swap(agg)
    w_n, w_s = pick_weights(core_at, agg, agg_swapped)
    cot_mine, cot_other = turn(core_at, cotangent, w_n)
    cot_swapped = swap(cot_other)
    weights = spread_ring(w_n, "y", NY) + spread_ring(w_s, "x", NX)

    there = sum(w[0, :8, :TILE] for w in weights[1:4] + weights[5:]) + cot_swapped[:8, :TILE]
    own_rows = hand_on(own_rows, (there, bias_here, place))
    act_mine, act_other, grads = layer(
        place, (agg, agg_swapped), (own_rows, swap(own_rows)), weights, bias_here, (cot_mine, cot_swapped)
    )
    pieces = lax.all_to_all(grads.reshape(32, PIECE, 768), ("y", "x", "core"), 0, 0)
    activation, token = unturn(core_at, act_mine, swap(act_other))
    summed = add_pieces(pieces, token)
    return activation, *add_last(lax.all_to_all(summed, "z", 0, 0))


def solution(mesh):
    split = Mesh(mesh.devices.reshape(NY, NX, NZ, NC), ("y", "x", "z", "core"))
    dp, feat = ("y", "x"), ("z", "core")
    every = dp + feat
    placed = (
        P(dp, feat), P(dp), P(dp, None), P(dp), P(dp, None, None, None),
        P(feat, None), P(feat, None), P(), P(every, None),
    )
    return jax.shard_map(
        shards,
        mesh=split,
        in_specs=placed,
        out_specs=(P(every, None), P(feat, dp), P(feat, dp)),
        check_vma=False,
    )
```

profile of v0, /device:TPU:32, one launch (start us, length us, event | category | flops | bytes accessed | tf_op | source)
XLA Modules:
  0.0 137.2 jit_solution(16326400713436697194)
XLA Ops:
  0.6 5.8 %aggregate.2.rest_0_ = bf16[8,48,1024]{2,1,0:T(8,128)(2,1)} custom-call(s32[4,64]{1,0:T(4,128)} %bitcast.14, s32[64]{0:T(128)} %count_ref.3, bf16[48,16384]{1,0:T(8,128)(2,1)} %bitcast.10, bf16[64,4,128,128]{3,2,1,0:T(8,128)(2,1)} %tiles_hbm.3, bf16[48,1024]{1,0:T(8,128)(2,1)} %rest_0_.1, bf16[48,1024]{1,0:T(8,128)(2,1)} %rest_1_.1), custom_call_target="tpu_custom_call" | custom-call | flops 200000000 | bytes 6000000 | tf_op jit(solution)/shard_map/aggregate/pallas_call | solution.py:82
  6.5 8.6 %all-to-all-start = ((bf16[8,48,1024]{2,1,0:T(8,128)(2,1)}), bf16[8,48,1024]{2,1,0:T(8,128)(2,1)S(1)}, u32[]{:S(2)}, u32[]{:S(2)}) async-start(bf16[8,48,1024]{2,1,0:T(8,128)(2,1)} %aggregate.2.rest_0_), calls=%async_computation | async-start | bytes 1572864 | tf_op jit(solution)/shard_map/all_to_all | solution.py:375
  15.1 5.5 %aggregate.3.agg_ref = bf16[8,48,512]{2,1,0:T(8,128)(2,1)} custom-call(s32[4,64]{1,0:T(4,128)} %bitcast.15, s32[64]{0:T(128)} %count_ref.3, bf16[48,16384]{1,0:T(8,128)(2,1)} %bitcast.11, bf16[64,4,128,128]{3,2,1,0:T(8,128)(2,1)} %tiles_hbm.3, bf16[8,48,1024]{2,1,0:T(8,128)(2,1)} %aggregate.2.rest_0_), custom_call_target="tpu_custom_call" | custom-call | flops 200000000 | bytes 6000000 | tf_op jit(solution)/shard_map/aggregate/pallas_call | solution.py:82
  21.6 13.2 %own_rows.1.refs_1_ = bf16[8,48,1536]{2,1,0:T(8,128)(2,1)} custom-call(s32[8192]{0:T(1024)S(1)} %copy-done.8, bf16[48,16384]{1,0:T(8,128)(2,1)S(1)} %bitcast.12, bf16[8,48,512]{2,1,0:T(8,128)(2,1)S(1)} %copy-done.3), custom_call_target="tpu_custom_call" | custom-call | bytes 60000000 | tf_op jit(solution)/shard_map/own_rows/pallas_call | solution.py:155
  34.8 1.9 %all-to-all-done.refs_0_ = bf16[8,48,1024]{2,1,0:T(8,128)(2,1)S(1)} async-done(((bf16[8,48,1024]{2,1,0:T(8,128)(2,1)}), bf16[8,48,1024]{2,1,0:T(8,128)(2,1)S(1)}, u32[]{:S(2)}, u32[]{:S(2)}) %all-to-all-start) | async-done | bytes 786464 | tf_op jit(solution)/shard_map/all_to_all | solution.py:375
  36.7 5.3 %all-to-all-start.1 = ((bf16[8,48,1536]{2,1,0:T(8,128)(2,1)}), bf16[8,48,1536]{2,1,0:T(8,128)(2,1)S(1)}, u32[]{:S(2)}, u32[]{:S(2)}) async-start(bf16[8,48,1536]{2,1,0:T(8,128)(2,1)} %own_rows.1.refs_1_), calls=%async_computation.1 | async-start | bytes 2359296 | tf_op jit(solution)/shard_map/all_to_all | solution.py:378
  42.1 2.4 %collective-permute-done.other_ref.agg_other = bf16[8,48,1024]{2,1,0:T(8,128)(2,1)} collective-permute-done((bf16[8,48,1024]{2,1,0:T(8,128)(2,1)S(1)}, bf16[8,48,1024]{2,1,0:T(8,128)(2,1)}, u32[]{:S(2)}, u32[]{:S(2)}) %collective-permute-start) | collective-permute-done | bytes 786464 | tf_op jit(solution)/shard_map/ppermute | solution.py:357
  44.5 1.3 pick_weights.1
  45.9 3.3 %turn_cotangent.1 = (bf16[512,512]{1,0:T(8,128)(2,1)S(1)}, bf16[512,512]{1,0:T(8,128)(2,1)}) custom-call(s32[1]{0:T(128)} %bitcast.core_ref, bf16[512,1024]{1,0:T(8,128)(2,1)S(1)} %copy-done.5, bf16[4,32,768]{2,1,0:T(8,128)(2,1)S(1)} %get-tuple-element.14.after_ref.n0), custom_call_target="tpu_custom_call" | custom-call | bytes 4000000 | tf_op jit(solution)/shard_map/turn_cotangent/pallas_call | solution.py:178
  50.1 2.8 %collective-permute-start.6 = (bf16[4,32,768]{2,1,0:T(8,128)(2,1)S(1)}, bf16[4,32,768]{2,1,0:T(8,128)(2,1)S(1)}, u32[]{:S(2)}, u32[]{:S(2)}) collective-permute-start(bf16[4,32,768]{2,1,0:T(8,128)(2,1)S(1)} %get-tuple-element.15.s0), channel_id=1, source_target_pairs={{0,48},{16,0},{32,16},{48,32},{1,49},{17,1},{33,17},{49,33},{2,50}... | collective-permute-start | bytes 589832 | tf_op jit(solution)/shard_map/ppermute | solution.py:362
  54.5 3.0 %collective-permute-start.3 = (bf16[4,32,768]{2,1,0:T(8,128)(2,1)S(1)}, bf16[4,32,768]{2,1,0:T(8,128)(2,1)}, u32[]{:S(2)}, u32[]{:S(2)}) collective-permute-start(bf16[4,32,768]{2,1,0:T(8,128)(2,1)S(1)} %get-tuple-element.14.after_ref.n0), channel_id=1, source_target_pairs={{0,192},{64,0},{128,64},{192,128},{1,193},{65,1},{129,65},{193,129... | collective-permute-start | bytes 589832 | tf_op jit(solution)/shard_map/ppermute | solution.py:362
  57.5 4.2 %collective-permute-done.6.s3 = bf16[4,32,768]{2,1,0:T(8,128)(2,1)S(1)} collective-permute-done((bf16[4,32,768]{2,1,0:T(8,128)(2,1)S(1)}, bf16[4,32,768]{2,1,0:T(8,128)(2,1)S(1)}, u32[]{:S(2)}, u32[]{:S(2)}) %collective-permute-start.6) | collective-permute-done | bytes 196640 | tf_op jit(solution)/shard_map/ppermute | solution.py:362
  61.8 3.2 %collective-permute-start.2 = (bf16[4,32,768]{2,1,0:T(8,128)(2,1)S(1)}, bf16[4,32,768]{2,1,0:T(8,128)(2,1)}, u32[]{:S(2)}, u32[]{:S(2)}) collective-permute-start(bf16[4,32,768]{2,1,0:T(8,128)(2,1)S(1)} %get-tuple-element.14.after_ref.n0), channel_id=1, source_target_pairs={{0,128},{64,192},{128,0},{192,64},{1,129},{65,193},{129,1},{193,65... | collective-permute-start | bytes 589832 | tf_op jit(solution)/shard_map/ppermute | solution.py:362
  66.2 5.1 %collective-permute-done.2.n2 = bf16[4,32,768]{2,1,0:T(8,128)(2,1)} collective-permute-done((bf16[4,32,768]{2,1,0:T(8,128)(2,1)S(1)}, bf16[4,32,768]{2,1,0:T(8,128)(2,1)}, u32[]{:S(2)}, u32[]{:S(2)}) %collective-permute-start.2) | collective-permute-done | bytes 196640 | tf_op jit(solution)/shard_map/ppermute | solution.py:362
  71.2 2.6 %collective-permute-done.1.n1 = bf16[4,32,768]{2,1,0:T(8,128)(2,1)} collective-permute-done((bf16[4,32,768]{2,1,0:T(8,128)(2,1)S(1)}, bf16[4,32,768]{2,1,0:T(8,128)(2,1)}, u32[]{:S(2)}, u32[]{:S(2)}) %collective-permute-start.1) | collective-permute-done | bytes 196640 | tf_op jit(solution)/shard_map/ppermute | solution.py:362
  74.7 2.8 %collective-permute-done.8.own_other = bf16[8,48,1536]{2,1,0:T(8,128)(2,1)S(1)} collective-permute-done((bf16[8,48,1536]{2,1,0:T(8,128)(2,1)S(1)}, bf16[8,48,1536]{2,1,0:T(8,128)(2,1)S(1)}, u32[]{:S(2)}, u32[]{:S(2)}) %collective-permute-start.8) | collective-permute-done | bytes 1179680 | tf_op jit(solution)/shard_map/ppermute | solution.py:357
  77.6 1.0 copy-done.16
  78.6 9.1 %layer.1 = (bf16[512,512]{1,0:T(8,128)(2,1)}, bf16[512,512]{1,0:T(8,128)(2,1)}, bf16[16,2,32,768]{3,2,1,0:T(8,128)(2,1)}) custom-call(s32[3]{0:T(128)} %copy-done.9, bf16[8,48,1024]{2,1,0:T(8,128)(2,1)} %copy-done.1, bf16[8,48,1024]{2,1,0:T(8,128)(2,1)} %collective-permute-done.other_ref.agg_other, bf16[8,48,1536]{2,1,0:T(8,128)(2,1)} %copy-done.2, ...), custom_call_target="tpu_custom_call" | custom-call | flops 3200000000 | bytes 9000000 | tf_op jit(solution)/shard_map/layer/pallas_call | solution.py:286
  87.7 7.5 %all-to-all-start.2 = ((bf16[32,32,768]{2,1,0:T(8,128)(2,1)}), bf16[32,32,768]{2,1,0:T(8,128)(2,1)S(1)}, u32[]{:S(2)}, u32[]{:S(2)}) async-start(bf16[32,32,768]{2,1,0:T(8,128)(2,1)} %bitcast.13), calls=%async_computation.2 | async-start | bytes 3145728 | tf_op jit(solution)/shard_map/all_to_all | solution.py:392
  95.6 1.6 %collective-permute-done.9.other_ref = bf16[512,512]{1,0:T(8,128)(2,1)S(1)} collective-permute-done((bf16[512,512]{1,0:T(8,128)(2,1)S(1)}, bf16[512,512]{1,0:T(8,128)(2,1)S(1)}, u32[]{:S(2)}, u32[]{:S(2)}) %collective-permute-start.9) | collective-permute-done | bytes 524320 | tf_op jit(solution)/shard_map/ppermute | solution.py:357
  97.2 3.2 %unturn_activation.1 = (bf16[512,1024]{1,0:T(8,128)(2,1)}, f32[8,128]{1,0:T(8,128)S(1)}) custom-call(s32[1]{0:T(128)} %bitcast.core_ref, bf16[512,512]{1,0:T(8,128)(2,1)S(1)} %copy-done.6, bf16[512,512]{1,0:T(8,128)(2,1)S(1)} %collective-permute-done.9.other_ref), custom_call_target="tpu_custom_call" | custom-call | bytes 4000000 | tf_op jit(solution)/shard_map/unturn_activation/pallas_call | solution.py:200
  100.4 18.8 %all-to-all-done.2.in_hbm = bf16[32,32,768]{2,1,0:T(8,128)(2,1)S(1)} async-done(((bf16[32,32,768]{2,1,0:T(8,128)(2,1)}), bf16[32,32,768]{2,1,0:T(8,128)(2,1)S(1)}, u32[]{:S(2)}, u32[]{:S(2)}) %all-to-all-start.2) | async-done | bytes 1572896 | tf_op jit(solution)/shard_map/all_to_all | solution.py:392
  119.1 2.7 %add_pieces.1 = bf16[8,64,96]{2,1,0:T(8,128)(2,1)S(1)} custom-call(bf16[32,32,768]{2,1,0:T(8,128)(2,1)S(1)} %all-to-all-done.2.in_hbm, f32[8,128]{1,0:T(8,128)S(1)} %get-tuple-element.22.token_ref), custom_call_target="tpu_custom_call" | custom-call | flops 800000 | bytes 1700000 | tf_op jit(solution)/shard_map/add_pieces/pallas_call | solution.py:322
  121.9 14.6 %all_to_all.20.in_ref = bf16[8,64,96]{2,1,0:T(8,128)(2,1)S(1)} all-to-all(bf16[8,64,96]{2,1,0:T(8,128)(2,1)S(1)} %add_pieces.1), channel_id=1, replica_groups=mesh['y'=4,'x'=4,'z'=8,'core'=2] {'z'}, dimensions={0} | all-to-all | bytes 196608 | tf_op jit(solution)/shard_map/all_to_all | solution.py:395
  (55 shorter events, 6.8 us)
Async XLA Ops:
  6.5 30.2 %all-to-all-start = ((bf16[8,48,1024]{2,1,0:T(8,128)(2,1)}), bf16[8,48,1024]{2,1,0:T(8,128)(2,1)S(1)}, u32[]{:S(2)}, u32[]{:S(2)}) async-start(bf16[8,48,1024]{2,1,0:T(8,128)(2,1)} %aggregate.2.rest_0_), calls=%async_computation | async-start | bytes 1572864 | tf_op jit(solution)/shard_map/all_to_all | solution.py:375
  36.7 37.8 %all-to-all-start.1 = ((bf16[8,48,1536]{2,1,0:T(8,128)(2,1)}), bf16[8,48,1536]{2,1,0:T(8,128)(2,1)S(1)}, u32[]{:S(2)}, u32[]{:S(2)}) async-start(bf16[8,48,1536]{2,1,0:T(8,128)(2,1)} %own_rows.1.refs_1_), calls=%async_computation.1 | async-start | bytes 2359296 | tf_op jit(solution)/shard_map/all_to_all | solution.py:378
  42.0 24.0 %copy-start.1 = (bf16[8,48,1024]{2,1,0:T(8,128)(2,1)}, bf16[8,48,1024]{2,1,0:T(8,128)(2,1)S(1)}, u32[]{:S(2)}) copy-start(bf16[8,48,1024]{2,1,0:T(8,128)(2,1)S(1)} %hand_on.2.mine_ref.agg_mine) | copy-start | bytes 2359300
  42.0 23.6 %copy-start.12 = (f32[1024]{0:T(1024)S(1)}, f32[1024]{0:T(1024)}, u32[]{:S(2)}) copy-start(f32[1024]{0:T(1024)} %param.16) | copy-start | bytes 12292
  42.0 2.5 %collective-permute-start = (bf16[8,48,1024]{2,1,0:T(8,128)(2,1)S(1)}, bf16[8,48,1024]{2,1,0:T(8,128)(2,1)}, u32[]{:S(2)}, u32[]{:S(2)}) collective-permute-start(bf16[8,48,1024]{2,1,0:T(8,128)(2,1)S(1)} %hand_on.2.mine_ref.agg_mine), channel_id=1, source_target_pairs={{0,1},{1,0},{2,3},{3,2},{4,5},{5,4},{6,7},{7,6},{8,9},{9,8},{10,11... | collective-permute-start | bytes 2359304 | tf_op jit(solution)/shard_map/ppermute | solution.py:357
  45.8 28.7 %copy-start.7 = (bf16[4,32,768]{2,1,0:T(8,128)(2,1)}, bf16[4,32,768]{2,1,0:T(8,128)(2,1)S(1)}, u32[]{:S(2)}) copy-start(bf16[4,32,768]{2,1,0:T(8,128)(2,1)S(1)} %get-tuple-element.14.after_ref.n0) | copy-start | bytes 589828
  45.9 28.7 %copy-start.11 = (bf16[4,32,768]{2,1,0:T(8,128)(2,1)}, bf16[4,32,768]{2,1,0:T(8,128)(2,1)S(1)}, u32[]{:S(2)}) copy-start(bf16[4,32,768]{2,1,0:T(8,128)(2,1)S(1)} %get-tuple-element.15.s0) | copy-start | bytes 589828
  49.9 23.9 %collective-permute-start.7 = (bf16[512,512]{1,0:T(8,128)(2,1)}, bf16[512,512]{1,0:T(8,128)(2,1)}, u32[]{:S(2)}, u32[]{:S(2)}) collective-permute-start(bf16[512,512]{1,0:T(8,128)(2,1)} %get-tuple-element.16), channel_id=1, source_target_pairs={{0,1},{1,0},{2,3},{3,2},{4,5},{5,4},{6,7},{7,6},{8,9},{9,8},{10,11... | collective-permute-start | bytes 1572872 | tf_op jit(solution)/shard_map/ppermute | solution.py:357
  50.1 11.7 %collective-permute-start.6 = (bf16[4,32,768]{2,1,0:T(8,128)(2,1)S(1)}, bf16[4,32,768]{2,1,0:T(8,128)(2,1)S(1)}, u32[]{:S(2)}, u32[]{:S(2)}) collective-permute-start(bf16[4,32,768]{2,1,0:T(8,128)(2,1)S(1)} %get-tuple-element.15.s0), channel_id=1, source_target_pairs={{0,48},{16,0},{32,16},{48,32},{1,49},{17,1},{33,17},{49,33},{2,50}... | collective-permute-start | bytes 589832 | tf_op jit(solution)/shard_map/ppermute | solution.py:362
  52.8 12.1 %collective-permute-start.5 = (bf16[4,32,768]{2,1,0:T(8,128)(2,1)S(1)}, bf16[4,32,768]{2,1,0:T(8,128)(2,1)S(1)}, u32[]{:S(2)}, u32[]{:S(2)}) collective-permute-start(bf16[4,32,768]{2,1,0:T(8,128)(2,1)S(1)} %get-tuple-element.15.s0), channel_id=1, source_target_pairs={{0,32},{16,48},{32,0},{48,16},{1,33},{17,49},{33,1},{49,17},{2,34}... | collective-permute-start | bytes 589832 | tf_op jit(solution)/shard_map/ppermute | solution.py:362
  53.6 12.5 %collective-permute-start.4 = (bf16[4,32,768]{2,1,0:T(8,128)(2,1)S(1)}, bf16[4,32,768]{2,1,0:T(8,128)(2,1)S(1)}, u32[]{:S(2)}, u32[]{:S(2)}) collective-permute-start(bf16[4,32,768]{2,1,0:T(8,128)(2,1)S(1)} %get-tuple-element.15.s0), channel_id=1, source_target_pairs={{0,16},{16,32},{32,48},{48,0},{1,17},{17,33},{33,49},{49,1},{2,18}... | collective-permute-start | bytes 589832 | tf_op jit(solution)/shard_map/ppermute | solution.py:362
  54.5 11.6 %collective-permute-start.3 = (bf16[4,32,768]{2,1,0:T(8,128)(2,1)S(1)}, bf16[4,32,768]{2,1,0:T(8,128)(2,1)}, u32[]{:S(2)}, u32[]{:S(2)}) collective-permute-start(bf16[4,32,768]{2,1,0:T(8,128)(2,1)S(1)} %get-tuple-element.14.after_ref.n0), channel_id=1, source_target_pairs={{0,192},{64,0},{128,64},{192,128},{1,193},{65,1},{129,65},{193,129... | collective-permute-start | bytes 589832 | tf_op jit(solution)/shard_map/ppermute | solution.py:362
  61.8 15.8 %copy-start.13 = (bf16[4,32,768]{2,1,0:T(8,128)(2,1)}, bf16[4,32,768]{2,1,0:T(8,128)(2,1)S(1)}, u32[]{:S(2)}) copy-start(bf16[4,32,768]{2,1,0:T(8,128)(2,1)S(1)} %collective-permute-done.6.s3) | copy-start | bytes 589828
  61.8 9.4 %collective-permute-start.2 = (bf16[4,32,768]{2,1,0:T(8,128)(2,1)S(1)}, bf16[4,32,768]{2,1,0:T(8,128)(2,1)}, u32[]{:S(2)}, u32[]{:S(2)}) collective-permute-start(bf16[4,32,768]{2,1,0:T(8,128)(2,1)S(1)} %get-tuple-element.14.after_ref.n0), channel_id=1, source_target_pairs={{0,128},{64,192},{128,0},{192,64},{1,129},{65,193},{129,1},{193,65... | collective-permute-start | bytes 589832 | tf_op jit(solution)/shard_map/ppermute | solution.py:362
  65.0 12.6 %copy-start.14 = (bf16[4,32,768]{2,1,0:T(8,128)(2,1)}, bf16[4,32,768]{2,1,0:T(8,128)(2,1)S(1)}, u32[]{:S(2)}) copy-start(bf16[4,32,768]{2,1,0:T(8,128)(2,1)S(1)} %collective-permute-done.5.s2) | copy-start | bytes 589828
  65.0 8.8 %collective-permute-start.1 = (bf16[4,32,768]{2,1,0:T(8,128)(2,1)S(1)}, bf16[4,32,768]{2,1,0:T(8,128)(2,1)}, u32[]{:S(2)}, u32[]{:S(2)}) collective-permute-start(bf16[4,32,768]{2,1,0:T(8,128)(2,1)S(1)} %get-tuple-element.14.after_ref.n0), channel_id=1, source_target_pairs={{0,64},{64,128},{128,192},{192,0},{1,65},{65,129},{129,193},{193,1... | collective-permute-start | bytes 589832 | tf_op jit(solution)/shard_map/ppermute | solution.py:362
  66.1 11.5 %copy-start.4 = (f32[512,1]{1,0:T(8,128)}, f32[512,1]{1,0:T(8,128)S(1)}, u32[]{:S(2)}) copy-start(f32[512,1]{1,0:T(8,128)S(1)} %reshape.28.refs_2_.bias_ref) | copy-start | bytes 6148
  66.1 11.4 %copy-start.9 = (s32[3]{0:T(128)}, s32[3]{0:T(128)S(1)}, u32[]{:S(2)}) copy-start(s32[3]{0:T(128)S(1)} %pad_add_fusion.refs_3_.place_ref) | copy-start | bytes 40
  66.1 11.4 %copy-start.15 = (bf16[4,32,768]{2,1,0:T(8,128)(2,1)}, bf16[4,32,768]{2,1,0:T(8,128)(2,1)S(1)}, u32[]{:S(2)}) copy-start(bf16[4,32,768]{2,1,0:T(8,128)(2,1)S(1)} %collective-permute-done.4.s1) | copy-start | bytes 589828
  74.6 2.9 %collective-permute-start.8 = (bf16[8,48,1536]{2,1,0:T(8,128)(2,1)S(1)}, bf16[8,48,1536]{2,1,0:T(8,128)(2,1)S(1)}, u32[]{:S(2)}, u32[]{:S(2)}) collective-permute-start(bf16[8,48,1536]{2,1,0:T(8,128)(2,1)S(1)} %hand_on.3.own_mine), channel_id=1, source_target_pairs={{0,1},{1,0},{2,3},{3,2},{4,5},{5,4},{6,7},{7,6},{8,9},{9,8},{10,11... | collective-permute-start | bytes 3538952 | tf_op jit(solution)/shard_map/ppermute | solution.py:357
  87.7 7.5 %copy-start.17 = (bf16[512,512]{1,0:T(8,128)(2,1)S(1)}, bf16[512,512]{1,0:T(8,128)(2,1)}, u32[]{:S(2)}) copy-start(bf16[512,512]{1,0:T(8,128)(2,1)} %get-tuple-element.19) | copy-start | bytes 1572868
  87.7 9.5 %copy-start.6 = (bf16[512,512]{1,0:T(8,128)(2,1)S(1)}, bf16[512,512]{1,0:T(8,128)(2,1)}, u32[]{:S(2)}) copy-start(bf16[512,512]{1,0:T(8,128)(2,1)} %get-tuple-element.18.mine_ref) | copy-start | bytes 1572868
  87.7 31.4 %all-to-all-start.2 = ((bf16[32,32,768]{2,1,0:T(8,128)(2,1)}), bf16[32,32,768]{2,1,0:T(8,128)(2,1)S(1)}, u32[]{:S(2)}, u32[]{:S(2)}) async-start(bf16[32,32,768]{2,1,0:T(8,128)(2,1)} %bitcast.13), calls=%async_computation.2 | async-start | bytes 3145728 | tf_op jit(solution)/shard_map/all_to_all | solution.py:392
  95.2 2.0 %collective-permute-start.9 = (bf16[512,512]{1,0:T(8,128)(2,1)S(1)}, bf16[512,512]{1,0:T(8,128)(2,1)S(1)}, u32[]{:S(2)}, u32[]{:S(2)}) collective-permute-start(bf16[512,512]{1,0:T(8,128)(2,1)S(1)} %copy-done.17), channel_id=1, source_target_pairs={{0,1},{1,0},{2,3},{3,2},{4,5},{5,4},{6,7},{7,6},{8,9},{9,8},{10,11... | collective-permute-start | bytes 1572872 | tf_op jit(solution)/shard_map/ppermute | solution.py:357
  (7 other events, 20.8 us)
where the time goes:
time: 138 us; the launch traced here: 137 us
  Pallas kernels  44.9 us (33%)
  waiting for transfers between devices  39.4 us (29%)
  starting transfers between devices  33.4 us (24%)
  blocking collectives  14.6 us (11%)
  local copies, waits for them, and re-layouts  3.21 us (2%)
    all_to_all x1, waiting for transfers between devices, shards(): lax.all_to_all(grads.reshape(32, PIECE, 768), ('y', 'x', 'core'), 0, 0)  18.8 us
    all_to_all x1, blocking collectives, shards(): return (activation, *add_last(lax.all_to_all(summed, 'z', 0, 0)))  14.6 us
    pallas_call x1, Pallas kernels, own(): pl.pallas_call(own_kernel, in_specs=[SMEM, VMEM, VMEM], out_specs=VMEM, o...  13.2 us
    ppermute x6, waiting for transfers between devices, spread_ring(): lax.ppermute(value, axis, [(i, (i + s) % size) for i in range(size)])  11.9 us
    pallas_call x2, Pallas kernels, aggregate(): pl.pallas_call(functools.partial(aggregate_kernel, half), in_specs=[SMEM,...  11.4 us
    ppermute x6, starting transfers between devices, spread_ring(): lax.ppermute(value, axis, [(i, (i + s) % size) for i in range(size)])  11.3 us
    pallas_call x1, Pallas kernels, layer(): pl.pallas_call(layer_kernel, in_specs=[SMEM] + [HBM] * 12 + [VMEM] + [HBM...  9.15 us
    all_to_all x1, starting transfers between devices, shards(): agg = lax.all_to_all(agg_sent, 'z', 0, 0)  8.58 us
  transfers between devices with their start and end apart: 13, of which 8 were waited for; matrix products, arithmetic and copies ran while one was open for 1% of the time, Pallas kernels for 19%

commit v1 on v0

--- a/solution.py
+++ b/solution.py
@@ -380,12 +380,12 @@
     agg = hand_on(agg, (own_sent,))
     agg_swapped = swap(agg)
     w_n, w_s = pick_weights(core_at, agg, agg_swapped)
-    cot_mine, cot_other = turn(core_at, cotangent, w_n)
+    weights = spread_ring(w_n, "y", NY) + spread_ring(w_s, "x", NX)
+
+    there = sum(w[0, :8, :TILE] for w in weights[1:4] + weights[5:])
+    cot_mine, cot_other = turn(core_at, cotangent, there)
     cot_swapped = swap(cot_other)
-    weights = spread_ring(w_n, "y", NY) + spread_ring(w_s, "x", NX)
-
-    there = sum(w[0, :8, :TILE] for w in weights[1:4] + weights[5:]) + cot_swapped[:8, :TILE]
-    own_rows = hand_on(own_rows, (there, bias_here, place))
+    own_rows = hand_on(own_rows, (there + cot_other[:8, :TILE], bias_here, place))
     act_mine, act_other, grads = layer(
         place, (agg, agg_swapped), (own_rows, swap(own_rows)), weights, bias_here, (cot_mine, cot_swapped)
     )

time: 138 us -> 134 us (0.971)
  blocking collectives: 14.6 us -> 11.9 us
  local copies, waits for them, and re-layouts: 3.21 us -> 4.91 us
  Pallas kernels: 44.9 us -> 43.5 us
    ppermute x6, waiting for transfers between devices: 11.9 us -> 9.03 us  [spread_ring(): lax.ppermute(value, axis, [(i, (i + s) % size) for i in range(size)])]
    all_to_all x1, blocking collectives: 14.6 us -> 11.9 us  [shards(): return (activation, *add_last(lax.all_to_all(summed, 'z', 0, 0)))]
    all_to_all x1, waiting for transfers between devices: 0.01 us -> 2.18 us  [shards(): own_rows = lax.all_to_all(own_sent, 'z', 0, 0)]
    pallas_call x1, Pallas kernels: 3.27 us -> 1.25 us  [turn(): pl.pallas_call(turn_kernel, grid=(8,), in_specs=[SMEM, pl.BlockSpec((HALF...]
    unnamed x36, local copies, waits for them, and re-layouts: 2.84 us -> 4.54 us
    ppermute x6, starting transfers between devices: 11.3 us -> 9.67 us  [spread_ring(): lax.ppermute(value, axis, [(i, (i + s) % size) for i in range(size)])]
  transfers between devices with their start and end apart: 13 -> 13, of which waited for: 8 -> 10; matrix products, arithmetic and copies ran while one was open for 1% -> 1% of each run, Pallas kernels for 19% -> 19%
where the time goes in v1:
time: 134 us; the launch traced here: 133 us
  Pallas kernels  43.5 us (32%)
  waiting for transfers between devices  39 us (29%)
  starting transfers between devices  32.1 us (24%)
  blocking collectives  11.9 us (9%)
  local copies, waits for them, and re-layouts  4.91 us (4%)
    all_to_all x1, waiting for transfers between devices, shards(): lax.all_to_all(grads.reshape(32, PIECE, 768), ('y', 'x', 'core'), 0, 0)  18.8 us
    pallas_call x1, Pallas kernels, own(): pl.pallas_call(own_kernel, in_specs=[SMEM, VMEM, VMEM], out_specs=VMEM, o...  13.2 us
    all_to_all x1, blocking collectives, shards(): return (activation, *add_last(lax.all_to_all(summed, 'z', 0, 0)))  11.9 us
    pallas_call x2, Pallas kernels, aggregate(): pl.pallas_call(functools.partial(aggregate_kernel, half), in_specs=[SMEM,...  11.4 us
    ppermute x6, starting transfers between devices, spread_ring(): lax.ppermute(value, axis, [(i, (i + s) % size) for i in range(size)])  9.67 us
    pallas_call x1, Pallas kernels, layer(): pl.pallas_call(layer_kernel, in_specs=[SMEM] + [HBM] * 12 + [VMEM] + [HBM...  9.14 us
    ppermute x6, waiting for transfers between devices, spread_ring(): lax.ppermute(value, axis, [(i, (i + s) % size) for i in range(size)])  9.03 us
    all_to_all x1, starting transfers between devices, shards(): agg = lax.all_to_all(agg_sent, 'z', 0, 0)  8.58 us
  transfers between devices with their start and end apart: 13, of which 10 were waited for; matrix products, arithmetic and copies ran while one was open for 1% of the time, Pallas kernels for 19%

profile of v1, /device:TPU:32, one launch (start us, length us, event | category | flops | bytes accessed | tf_op | source)
XLA Modules:
  0.0 133.0 jit_solution(10230330643739175093)
XLA Ops:
  0.6 5.8 %aggregate.2.rest_0_ = bf16[8,48,1024]{2,1,0:T(8,128)(2,1)} custom-call(s32[4,64]{1,0:T(4,128)} %bitcast.12, s32[64]{0:T(128)} %count_ref.3, bf16[48,16384]{1,0:T(8,128)(2,1)} %bitcast.8, bf16[64,4,128,128]{3,2,1,0:T(8,128)(2,1)} %tiles_hbm.3, bf16[48,1024]{1,0:T(8,128)(2,1)} %rest_0_.1, bf16[48,1024]{1,0:T(8,128)(2,1)} %rest_1_.1), custom_call_target="tpu_custom_call" | custom-call | flops 200000000 | bytes 6000000 | tf_op jit(solution)/shard_map/aggregate/pallas_call | solution.py:82
  6.5 8.6 %all-to-all-start = ((bf16[8,48,1024]{2,1,0:T(8,128)(2,1)}), bf16[8,48,1024]{2,1,0:T(8,128)(2,1)S(1)}, u32[]{:S(2)}, u32[]{:S(2)}) async-start(bf16[8,48,1024]{2,1,0:T(8,128)(2,1)} %aggregate.2.rest_0_), calls=%async_computation | async-start | bytes 1572864 | tf_op jit(solution)/shard_map/all_to_all | solution.py:375
  15.1 5.5 %aggregate.3.agg_ref = bf16[8,48,512]{2,1,0:T(8,128)(2,1)} custom-call(s32[4,64]{1,0:T(4,128)} %bitcast.13, s32[64]{0:T(128)} %count_ref.3, bf16[48,16384]{1,0:T(8,128)(2,1)} %bitcast.9, bf16[64,4,128,128]{3,2,1,0:T(8,128)(2,1)} %tiles_hbm.3, bf16[8,48,1024]{2,1,0:T(8,128)(2,1)} %aggregate.2.rest_0_), custom_call_target="tpu_custom_call" | custom-call | flops 200000000 | bytes 6000000 | tf_op jit(solution)/shard_map/aggregate/pallas_call | solution.py:82
  21.6 13.2 %own_rows.1.refs_1_ = bf16[8,48,1536]{2,1,0:T(8,128)(2,1)} custom-call(s32[8192]{0:T(1024)S(1)} %copy-done.7, bf16[48,16384]{1,0:T(8,128)(2,1)S(1)} %bitcast.10, bf16[8,48,512]{2,1,0:T(8,128)(2,1)S(1)} %copy-done.3), custom_call_target="tpu_custom_call" | custom-call | bytes 60000000 | tf_op jit(solution)/shard_map/own_rows/pallas_call | solution.py:155
  34.8 1.9 %all-to-all-done.refs_0_ = bf16[8,48,1024]{2,1,0:T(8,128)(2,1)S(1)} async-done(((bf16[8,48,1024]{2,1,0:T(8,128)(2,1)}), bf16[8,48,1024]{2,1,0:T(8,128)(2,1)S(1)}, u32[]{:S(2)}, u32[]{:S(2)}) %all-to-all-start) | async-done | bytes 786464 | tf_op jit(solution)/shard_map/all_to_all | solution.py:375
  36.7 5.3 %all-to-all-start.1 = ((bf16[8,48,1536]{2,1,0:T(8,128)(2,1)}), bf16[8,48,1536]{2,1,0:T(8,128)(2,1)S(1)}, u32[]{:S(2)}, u32[]{:S(2)}) async-start(bf16[8,48,1536]{2,1,0:T(8,128)(2,1)} %own_rows.1.refs_1_), calls=%async_computation.1 | async-start | bytes 2359296 | tf_op jit(solution)/shard_map/all_to_all | solution.py:378
  42.1 2.4 %collective-permute-done.other_ref.agg_other = bf16[8,48,1024]{2,1,0:T(8,128)(2,1)} collective-permute-done((bf16[8,48,1024]{2,1,0:T(8,128)(2,1)S(1)}, bf16[8,48,1024]{2,1,0:T(8,128)(2,1)}, u32[]{:S(2)}, u32[]{:S(2)}) %collective-permute-start) | collective-permute-done | bytes 786464 | tf_op jit(solution)/shard_map/ppermute | solution.py:357
  44.5 2.0 %pick_weights.1 = (bf16[4,32,768]{2,1,0:T(8,128)(2,1)S(1)}, bf16[4,32,768]{2,1,0:T(8,128)(2,1)}) custom-call(s32[1]{0:T(128)} %bitcast.core_ref, bf16[8,48,1024]{2,1,0:T(8,128)(2,1)S(1)} %hand_on.2.mine_ref.agg_mine, bf16[8,48,1024]{2,1,0:T(8,128)(2,1)} %collective-permute-done.other_ref.agg_other), custom_call_target="tpu_custom_call" | custom-call | bytes 1600000 | tf_op jit(solution)/shard_map/pick_weights/pallas_call | solution.py:114
  46.5 3.0 %collective-permute-start.3 = (bf16[4,32,768]{2,1,0:T(8,128)(2,1)S(1)}, bf16[4,32,768]{2,1,0:T(8,128)(2,1)S(1)}, u32[]{:S(2)}, u32[]{:S(2)}) collective-permute-start(bf16[4,32,768]{2,1,0:T(8,128)(2,1)S(1)} %get-tuple-element.14.n0), channel_id=1, source_target_pairs={{0,192},{64,0},{128,64},{192,128},{1,193},{65,1},{129,65},{193,129... | collective-permute-start | bytes 589832 | tf_op jit(solution)/shard_map/ppermute | solution.py:362
  51.1 2.8 %collective-permute-start.6 = (bf16[4,32,768]{2,1,0:T(8,128)(2,1)}, bf16[4,32,768]{2,1,0:T(8,128)(2,1)}, u32[]{:S(2)}, u32[]{:S(2)}) collective-permute-start(bf16[4,32,768]{2,1,0:T(8,128)(2,1)} %get-tuple-element.15.s0), channel_id=1, source_target_pairs={{0,48},{16,0},{32,16},{48,32},{1,49},{17,1},{33,17},{49,33},{2,50}... | collective-permute-start | bytes 589832 | tf_op jit(solution)/shard_map/ppermute | solution.py:362
  54.7 3.5 %collective-permute-done.3.n3 = bf16[4,32,768]{2,1,0:T(8,128)(2,1)S(1)} collective-permute-done((bf16[4,32,768]{2,1,0:T(8,128)(2,1)S(1)}, bf16[4,32,768]{2,1,0:T(8,128)(2,1)S(1)}, u32[]{:S(2)}, u32[]{:S(2)}) %collective-permute-start.3) | collective-permute-done | bytes 196640 | tf_op jit(solution)/shard_map/ppermute | solution.py:362
  58.9 1.5 %collective-permute-start.4 = (bf16[4,32,768]{2,1,0:T(8,128)(2,1)}, bf16[4,32,768]{2,1,0:T(8,128)(2,1)}, u32[]{:S(2)}, u32[]{:S(2)}) collective-permute-start(bf16[4,32,768]{2,1,0:T(8,128)(2,1)} %get-tuple-element.15.s0), channel_id=1, source_target_pairs={{0,16},{16,32},{32,48},{48,0},{1,17},{17,33},{33,49},{49,1},{2,18}... | collective-permute-start | bytes 589832 | tf_op jit(solution)/shard_map/ppermute | solution.py:362
  60.9 1.1 collective-permute-done.1.n1
  62.1 4.3 %collective-permute-done.4.s1 = bf16[4,32,768]{2,1,0:T(8,128)(2,1)} collective-permute-done((bf16[4,32,768]{2,1,0:T(8,128)(2,1)}, bf16[4,32,768]{2,1,0:T(8,128)(2,1)}, u32[]{:S(2)}, u32[]{:S(2)}) %collective-permute-start.4) | collective-permute-done | bytes 196640 | tf_op jit(solution)/shard_map/ppermute | solution.py:362
  67.1 1.3 turn_cotangent.1
  70.0 2.2 %all-to-all-done.1.refs_0_ = bf16[8,48,1536]{2,1,0:T(8,128)(2,1)S(1)} async-done(((bf16[8,48,1536]{2,1,0:T(8,128)(2,1)}), bf16[8,48,1536]{2,1,0:T(8,128)(2,1)S(1)}, u32[]{:S(2)}, u32[]{:S(2)}) %all-to-all-start.1) | async-done | bytes 1179680 | tf_op jit(solution)/shard_map/all_to_all | solution.py:378
  72.8 3.1 %collective-permute-done.8.cot_other = bf16[512,512]{1,0:T(8,128)(2,1)S(1)} collective-permute-done((bf16[512,512]{1,0:T(8,128)(2,1)S(1)}, bf16[512,512]{1,0:T(8,128)(2,1)S(1)}, u32[]{:S(2)}, u32[]{:S(2)}) %collective-permute-start.8) | collective-permute-done | bytes 524320 | tf_op jit(solution)/shard_map/ppermute | solution.py:357
  77.1 9.1 %layer.1 = (bf16[512,512]{1,0:T(8,128)(2,1)}, bf16[512,512]{1,0:T(8,128)(2,1)}, bf16[16,2,32,768]{3,2,1,0:T(8,128)(2,1)}) custom-call(s32[3]{0:T(128)} %copy-done.8, bf16[8,48,1024]{2,1,0:T(8,128)(2,1)} %copy-done.1, bf16[8,48,1024]{2,1,0:T(8,128)(2,1)} %collective-permute-done.other_ref.agg_other, bf16[8,48,1536]{2,1,0:T(8,128)(2,1)} %copy-done.2, ...), custom_call_target="tpu_custom_call" | custom-call | flops 3200000000 | bytes 9000000 | tf_op jit(solution)/shard_map/layer/pallas_call | solution.py:286
  86.3 7.5 %all-to-all-start.2 = ((bf16[32,32,768]{2,1,0:T(8,128)(2,1)}), bf16[32,32,768]{2,1,0:T(8,128)(2,1)S(1)}, u32[]{:S(2)}, u32[]{:S(2)}) async-start(bf16[32,32,768]{2,1,0:T(8,128)(2,1)} %bitcast.11), calls=%async_computation.2 | async-start | bytes 3145728 | tf_op jit(solution)/shard_map/all_to_all | solution.py:392
  94.1 1.6 %collective-permute-done.9.other_ref = bf16[512,512]{1,0:T(8,128)(2,1)S(1)} collective-permute-done((bf16[512,512]{1,0:T(8,128)(2,1)S(1)}, bf16[512,512]{1,0:T(8,128)(2,1)S(1)}, u32[]{:S(2)}, u32[]{:S(2)}) %collective-permute-start.9) | collective-permute-done | bytes 524320 | tf_op jit(solution)/shard_map/ppermute | solution.py:357
  95.8 3.2 %unturn_activation.1 = (bf16[512,1024]{1,0:T(8,128)(2,1)}, f32[8,128]{1,0:T(8,128)S(1)}) custom-call(s32[1]{0:T(128)} %bitcast.core_ref, bf16[512,512]{1,0:T(8,128)(2,1)S(1)} %copy-done.6, bf16[512,512]{1,0:T(8,128)(2,1)S(1)} %collective-permute-done.9.other_ref), custom_call_target="tpu_custom_call" | custom-call | bytes 4000000 | tf_op jit(solution)/shard_map/unturn_activation/pallas_call | solution.py:200
  98.9 18.8 %all-to-all-done.2.in_hbm = bf16[32,32,768]{2,1,0:T(8,128)(2,1)S(1)} async-done(((bf16[32,32,768]{2,1,0:T(8,128)(2,1)}), bf16[32,32,768]{2,1,0:T(8,128)(2,1)S(1)}, u32[]{:S(2)}, u32[]{:S(2)}) %all-to-all-start.2) | async-done | bytes 1572896 | tf_op jit(solution)/shard_map/all_to_all | solution.py:392
  117.7 2.7 %add_pieces.1 = bf16[8,64,96]{2,1,0:T(8,128)(2,1)S(1)} custom-call(bf16[32,32,768]{2,1,0:T(8,128)(2,1)S(1)} %all-to-all-done.2.in_hbm, f32[8,128]{1,0:T(8,128)S(1)} %get-tuple-element.22.token_ref), custom_call_target="tpu_custom_call" | custom-call | flops 800000 | bytes 1700000 | tf_op jit(solution)/shard_map/add_pieces/pallas_call | solution.py:322
  120.4 11.9 %all_to_all.20.in_ref = bf16[8,64,96]{2,1,0:T(8,128)(2,1)S(1)} all-to-all(bf16[8,64,96]{2,1,0:T(8,128)(2,1)S(1)} %add_pieces.1), channel_id=1, replica_groups=mesh['y'=4,'x'=4,'z'=8,'core'=2] {'z'}, dimensions={0} | all-to-all | bytes 196608 | tf_op jit(solution)/shard_map/all_to_all | solution.py:395
  (56 shorter events, 9.9 us)
Async XLA Ops:
  6.5 30.2 %all-to-all-start = ((bf16[8,48,1024]{2,1,0:T(8,128)(2,1)}), bf16[8,48,1024]{2,1,0:T(8,128)(2,1)S(1)}, u32[]{:S(2)}, u32[]{:S(2)}) async-start(bf16[8,48,1024]{2,1,0:T(8,128)(2,1)} %aggregate.2.rest_0_), calls=%async_computation | async-start | bytes 1572864 | tf_op jit(solution)/shard_map/all_to_all | solution.py:375
  15.0 5.6 %copy-start = (bf16[16384,48]{0,1:T(8,128)(2,1)S(1)}, bf16[16384,48]{0,1:T(8,128)(2,1)}, u32[]{:S(2)}) copy-start(bf16[16384,48]{0,1:T(8,128)(2,1)} %param.9) | copy-start | bytes 4718596
  15.1 5.6 %copy-start.7 = (s32[8192]{0:T(1024)S(1)}, s32[8192]{0:T(1024)}, u32[]{:S(2)}) copy-start(s32[8192]{0:T(1024)} %ids_ref.1) | copy-start | bytes 98308
  36.7 35.5 %all-to-all-start.1 = ((bf16[8,48,1536]{2,1,0:T(8,128)(2,1)}), bf16[8,48,1536]{2,1,0:T(8,128)(2,1)S(1)}, u32[]{:S(2)}, u32[]{:S(2)}) async-start(bf16[8,48,1536]{2,1,0:T(8,128)(2,1)} %own_rows.1.refs_1_), calls=%async_computation.1 | async-start | bytes 2359296 | tf_op jit(solution)/shard_map/all_to_all | solution.py:378
  42.0 18.4 %copy-start.13 = (f32[1024]{0:T(1024)S(1)}, f32[1024]{0:T(1024)}, u32[]{:S(2)}) copy-start(f32[1024]{0:T(1024)} %param.16) | copy-start | bytes 12292
  42.0 30.2 %copy-start.1 = (bf16[8,48,1024]{2,1,0:T(8,128)(2,1)}, bf16[8,48,1024]{2,1,0:T(8,128)(2,1)S(1)}, u32[]{:S(2)}) copy-start(bf16[8,48,1024]{2,1,0:T(8,128)(2,1)S(1)} %hand_on.2.mine_ref.agg_mine) | copy-start | bytes 2359300
  42.0 25.1 %copy-start.5 = (bf16[512,1024]{1,0:T(8,128)(2,1)S(1)}, bf16[512,1024]{1,0:T(8,128)(2,1)}, u32[]{:S(2)}) copy-start(bf16[512,1024]{1,0:T(8,128)(2,1)} %cot_ref.1) | copy-start | bytes 3145732
  42.0 2.5 %collective-permute-start = (bf16[8,48,1024]{2,1,0:T(8,128)(2,1)S(1)}, bf16[8,48,1024]{2,1,0:T(8,128)(2,1)}, u32[]{:S(2)}, u32[]{:S(2)}) collective-permute-start(bf16[8,48,1024]{2,1,0:T(8,128)(2,1)S(1)} %hand_on.2.mine_ref.agg_mine), channel_id=1, source_target_pairs={{0,1},{1,0},{2,3},{3,2},{4,5},{5,4},{6,7},{7,6},{8,9},{9,8},{10,11... | collective-permute-start | bytes 2359304 | tf_op jit(solution)/shard_map/ppermute | solution.py:357
  46.5 25.7 %copy-start.12 = (bf16[4,32,768]{2,1,0:T(8,128)(2,1)}, bf16[4,32,768]{2,1,0:T(8,128)(2,1)S(1)}, u32[]{:S(2)}) copy-start(bf16[4,32,768]{2,1,0:T(8,128)(2,1)S(1)} %get-tuple-element.14.n0) | copy-start | bytes 589828
  46.5 11.7 %collective-permute-start.3 = (bf16[4,32,768]{2,1,0:T(8,128)(2,1)S(1)}, bf16[4,32,768]{2,1,0:T(8,128)(2,1)S(1)}, u32[]{:S(2)}, u32[]{:S(2)}) collective-permute-start(bf16[4,32,768]{2,1,0:T(8,128)(2,1)S(1)} %get-tuple-element.14.n0), channel_id=1, source_target_pairs={{0,192},{64,0},{128,64},{192,128},{1,193},{65,1},{129,65},{193,129... | collective-permute-start | bytes 589832 | tf_op jit(solution)/shard_map/ppermute | solution.py:362
  49.5 11.3 %collective-permute-start.2 = (bf16[4,32,768]{2,1,0:T(8,128)(2,1)S(1)}, bf16[4,32,768]{2,1,0:T(8,128)(2,1)}, u32[]{:S(2)}, u32[]{:S(2)}) collective-permute-start(bf16[4,32,768]{2,1,0:T(8,128)(2,1)S(1)} %get-tuple-element.14.n0), channel_id=1, source_target_pairs={{0,128},{64,192},{128,0},{192,64},{1,129},{65,193},{129,1},{193,65... | collective-permute-start | bytes 589832 | tf_op jit(solution)/shard_map/ppermute | solution.py:362
  50.1 11.9 %collective-permute-start.1 = (bf16[4,32,768]{2,1,0:T(8,128)(2,1)S(1)}, bf16[4,32,768]{2,1,0:T(8,128)(2,1)}, u32[]{:S(2)}, u32[]{:S(2)}) collective-permute-start(bf16[4,32,768]{2,1,0:T(8,128)(2,1)S(1)} %get-tuple-element.14.n0), channel_id=1, source_target_pairs={{0,64},{64,128},{128,192},{192,0},{1,65},{65,129},{129,193},{193,1... | collective-permute-start | bytes 589832 | tf_op jit(solution)/shard_map/ppermute | solution.py:362
  51.1 10.9 %collective-permute-start.6 = (bf16[4,32,768]{2,1,0:T(8,128)(2,1)}, bf16[4,32,768]{2,1,0:T(8,128)(2,1)}, u32[]{:S(2)}, u32[]{:S(2)}) collective-permute-start(bf16[4,32,768]{2,1,0:T(8,128)(2,1)} %get-tuple-element.15.s0), channel_id=1, source_target_pairs={{0,48},{16,0},{32,16},{48,32},{1,49},{17,1},{33,17},{49,33},{2,50}... | collective-permute-start | bytes 589832 | tf_op jit(solution)/shard_map/ppermute | solution.py:362
  53.9 8.2 %collective-permute-start.5 = (bf16[4,32,768]{2,1,0:T(8,128)(2,1)}, bf16[4,32,768]{2,1,0:T(8,128)(2,1)}, u32[]{:S(2)}, u32[]{:S(2)}) collective-permute-start(bf16[4,32,768]{2,1,0:T(8,128)(2,1)} %get-tuple-element.15.s0), channel_id=1, source_target_pairs={{0,32},{16,48},{32,0},{48,16},{1,33},{17,49},{33,1},{49,17},{2,34}... | collective-permute-start | bytes 589832 | tf_op jit(solution)/shard_map/ppermute | solution.py:362
  58.9 7.5 %collective-permute-start.4 = (bf16[4,32,768]{2,1,0:T(8,128)(2,1)}, bf16[4,32,768]{2,1,0:T(8,128)(2,1)}, u32[]{:S(2)}, u32[]{:S(2)}) collective-permute-start(bf16[4,32,768]{2,1,0:T(8,128)(2,1)} %get-tuple-element.15.s0), channel_id=1, source_target_pairs={{0,16},{16,32},{32,48},{48,0},{1,17},{17,33},{33,49},{49,1},{2,18}... | collective-permute-start | bytes 589832 | tf_op jit(solution)/shard_map/ppermute | solution.py:362
  60.8 11.4 %copy-start.4 = (f32[512,1]{1,0:T(8,128)}, f32[512,1]{1,0:T(8,128)S(1)}, u32[]{:S(2)}) copy-start(f32[512,1]{1,0:T(8,128)S(1)} %reshape.28.refs_2_.bias_ref) | copy-start | bytes 6148
  60.9 11.4 %copy-start.8 = (s32[3]{0:T(128)}, s32[3]{0:T(128)S(1)}, u32[]{:S(2)}) copy-start(s32[3]{0:T(128)S(1)} %pad_add_fusion.refs_3_.place_ref) | copy-start | bytes 40
  72.2 3.7 %copy-start.2 = (bf16[8,48,1536]{2,1,0:T(8,128)(2,1)}, bf16[8,48,1536]{2,1,0:T(8,128)(2,1)S(1)}, u32[]{:S(2)}) copy-start(bf16[8,48,1536]{2,1,0:T(8,128)(2,1)S(1)} %hand_on.3.own_mine) | copy-start | bytes 3538948
  72.2 3.7 %collective-permute-start.7 = (bf16[8,48,1536]{2,1,0:T(8,128)(2,1)S(1)}, bf16[8,48,1536]{2,1,0:T(8,128)(2,1)S(1)}, u32[]{:S(2)}, u32[]{:S(2)}) collective-permute-start(bf16[8,48,1536]{2,1,0:T(8,128)(2,1)S(1)} %hand_on.3.own_mine), channel_id=1, source_target_pairs={{0,1},{1,0},{2,3},{3,2},{4,5},{5,4},{6,7},{7,6},{8,9},{9,8},{10,11... | collective-permute-start | bytes 3538952 | tf_op jit(solution)/shard_map/ppermute | solution.py:357
  72.3 3.6 %collective-permute-start.8 = (bf16[512,512]{1,0:T(8,128)(2,1)S(1)}, bf16[512,512]{1,0:T(8,128)(2,1)S(1)}, u32[]{:S(2)}, u32[]{:S(2)}) collective-permute-start(bf16[512,512]{1,0:T(8,128)(2,1)S(1)} %copy-done.10), channel_id=1, source_target_pairs={{0,1},{1,0},{2,3},{3,2},{4,5},{5,4},{6,7},{7,6},{8,9},{9,8},{10,11... | collective-permute-start | bytes 1572872 | tf_op jit(solution)/shard_map/ppermute | solution.py:357
  86.3 7.5 %copy-start.16 = (bf16[512,512]{1,0:T(8,128)(2,1)S(1)}, bf16[512,512]{1,0:T(8,128)(2,1)}, u32[]{:S(2)}) copy-start(bf16[512,512]{1,0:T(8,128)(2,1)} %get-tuple-element.19) | copy-start | bytes 1572868
  86.3 9.5 %copy-start.6 = (bf16[512,512]{1,0:T(8,128)(2,1)S(1)}, bf16[512,512]{1,0:T(8,128)(2,1)}, u32[]{:S(2)}) copy-start(bf16[512,512]{1,0:T(8,128)(2,1)} %get-tuple-element.18.mine_ref) | copy-start | bytes 1572868
  86.3 31.4 %all-to-all-start.2 = ((bf16[32,32,768]{2,1,0:T(8,128)(2,1)}), bf16[32,32,768]{2,1,0:T(8,128)(2,1)S(1)}, u32[]{:S(2)}, u32[]{:S(2)}) async-start(bf16[32,32,768]{2,1,0:T(8,128)(2,1)} %bitcast.11), calls=%async_computation.2 | async-start | bytes 3145728 | tf_op jit(solution)/shard_map/all_to_all | solution.py:392
  93.8 2.0 %collective-permute-start.9 = (bf16[512,512]{1,0:T(8,128)(2,1)S(1)}, bf16[512,512]{1,0:T(8,128)(2,1)S(1)}, u32[]{:S(2)}, u32[]{:S(2)}) collective-permute-start(bf16[512,512]{1,0:T(8,128)(2,1)S(1)} %copy-done.16), channel_id=1, source_target_pairs={{0,1},{1,0},{2,3},{3,2},{4,5},{5,4},{6,7},{7,6},{8,9},{9,8},{10,11... | collective-permute-start | bytes 1572872 | tf_op jit(solution)/shard_map/ppermute | solution.py:357
  (7 other events, 7.6 us)

commit v2 on v1

--- a/solution.py
+++ b/solution.py
@@ -303,14 +303,10 @@
     )(place, *aggs, *owns, *weights, bias, *cots)
 
 
-def add_kernel(in_hbm, token_ref, out_ref, held, sems):
-    copies = [pltpu.make_async_copy(in_hbm.at[i], held.at[i], sems.at[i]) for i in range(32)]
-    for copy in copies:
-        copy.start()
+def add_kernel(in_ref, token_ref, out_ref):
     totals = [None, None]
-    for i, copy in enumerate(copies):
-        copy.wait()
-        term = held[i].astype(F32)
+    for i in range(32):
+        term = in_ref[i].astype(F32)
         totals[i % 2] = term if totals[i % 2] is None else totals[i % 2] + term
     total = jnp.concatenate(totals, axis=0)
     for z in range(NZ):
@@ -321,10 +317,9 @@
 def add_pieces(pieces, token):
     return pl.pallas_call(
         add_kernel,
-        in_specs=[ANY, ANY],
+        in_specs=[VMEM, ANY],
         out_specs=VMEM,
         out_shape=jax.ShapeDtypeStruct((NZ, 64, 2 * COLS), BF),
-        scratch_shapes=[pltpu.VMEM((32, PIECE, 768), BF), pltpu.SemaphoreType.DMA((32,))],
         compiler_params=params(8),
         cost_estimate=pl.CostEstimate(flops=800_000, bytes_accessed=1_700_000, transcendentals=0),
         name="add_pieces",

time: 134 us -> 131 us (0.978)
  Pallas kernels: 43.5 us -> 41.1 us
    pallas_call x1, Pallas kernels: 2.73 us -> 0.32 us  [add_pieces(): pl.pallas_call(add_kernel, in_specs=[VMEM, ANY], out_specs=VMEM, out_shap...]
where the time goes in v2:
time: 131 us
  Pallas kernels  41.1 us (31%)
  waiting for transfers between devices  39 us (30%)
  starting transfers between devices  32 us (24%)
  blocking collectives  11.9 us (9%)
  local copies, waits for them, and re-layouts  4.91 us (4%)
    all_to_all x1, waiting for transfers between devices, shards(): lax.all_to_all(grads.reshape(32, PIECE, 768), ('y', 'x', 'core'), 0, 0)  18.8 us
    pallas_call x1, Pallas kernels, own(): pl.pallas_call(own_kernel, in_specs=[SMEM, VMEM, VMEM], out_specs=VMEM, o...  13.2 us
    all_to_all x1, blocking collectives, shards(): return (activation, *add_last(lax.all_to_all(summed, 'z', 0, 0)))  11.9 us
    pallas_call x2, Pallas kernels, aggregate(): pl.pallas_call(functools.partial(aggregate_kernel, half), in_specs=[SMEM,...  11.4 us
    ppermute x6, starting transfers between devices, spread_ring(): lax.ppermute(value, axis, [(i, (i + s) % size) for i in range(size)])  9.66 us
    pallas_call x1, Pallas kernels, layer(): pl.pallas_call(layer_kernel, in_specs=[SMEM] + [HBM] * 12 + [VMEM] + [HBM...  9.14 us
    ppermute x6, waiting for transfers between devices, spread_ring(): lax.ppermute(value, axis, [(i, (i + s) % size) for i in range(size)])  9.06 us
    all_to_all x1, starting transfers between devices, shards(): agg = lax.all_to_all(agg_sent, 'z', 0, 0)  8.58 us
  transfers between devices with their start and end apart: 13, of which 10 were waited for; matrix products, arithmetic and copies ran while one was open for 1% of the time, Pallas kernels for 19%

profile of v2, /device:TPU:32, one launch (start us, length us, event | category | flops | bytes accessed | tf_op | source)
XLA Modules:
  0.0 130.6 jit_solution(12593125048032710374)
XLA Ops:
  0.6 5.8 %aggregate.2.rest_0_ = bf16[8,48,1024]{2,1,0:T(8,128)(2,1)} custom-call(s32[4,64]{1,0:T(4,128)} %bitcast.12, s32[64]{0:T(128)} %count_ref.3, bf16[48,16384]{1,0:T(8,128)(2,1)} %bitcast.8, bf16[64,4,128,128]{3,2,1,0:T(8,128)(2,1)} %tiles_hbm.3, bf16[48,1024]{1,0:T(8,128)(2,1)} %rest_0_.1, bf16[48,1024]{1,0:T(8,128)(2,1)} %rest_1_.1), custom_call_target="tpu_custom_call" | custom-call | flops 200000000 | bytes 6000000 | tf_op jit(solution)/shard_map/aggregate/pallas_call | solution.py:82
  6.5 8.6 %all-to-all-start = ((bf16[8,48,1024]{2,1,0:T(8,128)(2,1)}), bf16[8,48,1024]{2,1,0:T(8,128)(2,1)S(1)}, u32[]{:S(2)}, u32[]{:S(2)}) async-start(bf16[8,48,1024]{2,1,0:T(8,128)(2,1)} %aggregate.2.rest_0_), calls=%async_computation | async-start | bytes 1572864 | tf_op jit(solution)/shard_map/all_to_all | solution.py:370
  15.1 5.5 %aggregate.3.agg_ref = bf16[8,48,512]{2,1,0:T(8,128)(2,1)} custom-call(s32[4,64]{1,0:T(4,128)} %bitcast.13, s32[64]{0:T(128)} %count_ref.3, bf16[48,16384]{1,0:T(8,128)(2,1)} %bitcast.9, bf16[64,4,128,128]{3,2,1,0:T(8,128)(2,1)} %tiles_hbm.3, bf16[8,48,1024]{2,1,0:T(8,128)(2,1)} %aggregate.2.rest_0_), custom_call_target="tpu_custom_call" | custom-call | flops 200000000 | bytes 6000000 | tf_op jit(solution)/shard_map/aggregate/pallas_call | solution.py:82
  20.6 1.0 copy-done.3
  21.6 13.2 %own_rows.1.refs_1_ = bf16[8,48,1536]{2,1,0:T(8,128)(2,1)} custom-call(s32[8192]{0:T(1024)S(1)} %copy-done.7, bf16[48,16384]{1,0:T(8,128)(2,1)S(1)} %bitcast.10, bf16[8,48,512]{2,1,0:T(8,128)(2,1)S(1)} %copy-done.3), custom_call_target="tpu_custom_call" | custom-call | bytes 60000000 | tf_op jit(solution)/shard_map/own_rows/pallas_call | solution.py:155
  34.8 1.9 %all-to-all-done.refs_0_ = bf16[8,48,1024]{2,1,0:T(8,128)(2,1)S(1)} async-done(((bf16[8,48,1024]{2,1,0:T(8,128)(2,1)}), bf16[8,48,1024]{2,1,0:T(8,128)(2,1)S(1)}, u32[]{:S(2)}, u32[]{:S(2)}) %all-to-all-start) | async-done | bytes 786464 | tf_op jit(solution)/shard_map/all_to_all | solution.py:370
  36.7 5.3 %all-to-all-start.1 = ((bf16[8,48,1536]{2,1,0:T(8,128)(2,1)}), bf16[8,48,1536]{2,1,0:T(8,128)(2,1)S(1)}, u32[]{:S(2)}, u32[]{:S(2)}) async-start(bf16[8,48,1536]{2,1,0:T(8,128)(2,1)} %own_rows.1.refs_1_), calls=%async_computation.1 | async-start | bytes 2359296 | tf_op jit(solution)/shard_map/all_to_all | solution.py:373
  42.1 2.4 %collective-permute-done.other_ref.agg_other = bf16[8,48,1024]{2,1,0:T(8,128)(2,1)} collective-permute-done((bf16[8,48,1024]{2,1,0:T(8,128)(2,1)S(1)}, bf16[8,48,1024]{2,1,0:T(8,128)(2,1)}, u32[]{:S(2)}, u32[]{:S(2)}) %collective-permute-start) | collective-permute-done | bytes 786464 | tf_op jit(solution)/shard_map/ppermute | solution.py:352
  44.5 2.0 %pick_weights.1 = (bf16[4,32,768]{2,1,0:T(8,128)(2,1)S(1)}, bf16[4,32,768]{2,1,0:T(8,128)(2,1)}) custom-call(s32[1]{0:T(128)} %bitcast.core_ref, bf16[8,48,1024]{2,1,0:T(8,128)(2,1)S(1)} %hand_on.2.mine_ref.agg_mine, bf16[8,48,1024]{2,1,0:T(8,128)(2,1)} %collective-permute-done.other_ref.agg_other), custom_call_target="tpu_custom_call" | custom-call | bytes 1600000 | tf_op jit(solution)/shard_map/pick_weights/pallas_call | solution.py:114
  46.5 3.0 %collective-permute-start.3 = (bf16[4,32,768]{2,1,0:T(8,128)(2,1)S(1)}, bf16[4,32,768]{2,1,0:T(8,128)(2,1)S(1)}, u32[]{:S(2)}, u32[]{:S(2)}) collective-permute-start(bf16[4,32,768]{2,1,0:T(8,128)(2,1)S(1)} %get-tuple-element.14.n0), channel_id=1, source_target_pairs={{0,192},{64,0},{128,64},{192,128},{1,193},{65,1},{129,65},{193,129... | collective-permute-start | bytes 589832 | tf_op jit(solution)/shard_map/ppermute | solution.py:357
  51.1 2.8 %collective-permute-start.6 = (bf16[4,32,768]{2,1,0:T(8,128)(2,1)}, bf16[4,32,768]{2,1,0:T(8,128)(2,1)}, u32[]{:S(2)}, u32[]{:S(2)}) collective-permute-start(bf16[4,32,768]{2,1,0:T(8,128)(2,1)} %get-tuple-element.15.s0), channel_id=1, source_target_pairs={{0,48},{16,0},{32,16},{48,32},{1,49},{17,1},{33,17},{49,33},{2,50}... | collective-permute-start | bytes 589832 | tf_op jit(solution)/shard_map/ppermute | solution.py:357
  54.7 3.5 %collective-permute-done.3.n3 = bf16[4,32,768]{2,1,0:T(8,128)(2,1)S(1)} collective-permute-done((bf16[4,32,768]{2,1,0:T(8,128)(2,1)S(1)}, bf16[4,32,768]{2,1,0:T(8,128)(2,1)S(1)}, u32[]{:S(2)}, u32[]{:S(2)}) %collective-permute-start.3) | collective-permute-done | bytes 196640 | tf_op jit(solution)/shard_map/ppermute | solution.py:357
  58.9 1.5 %collective-permute-start.4 = (bf16[4,32,768]{2,1,0:T(8,128)(2,1)}, bf16[4,32,768]{2,1,0:T(8,128)(2,1)}, u32[]{:S(2)}, u32[]{:S(2)}) collective-permute-start(bf16[4,32,768]{2,1,0:T(8,128)(2,1)} %get-tuple-element.15.s0), channel_id=1, source_target_pairs={{0,16},{16,32},{32,48},{48,0},{1,17},{17,33},{33,49},{49,1},{2,18}... | collective-permute-start | bytes 589832 | tf_op jit(solution)/shard_map/ppermute | solution.py:357
  60.9 1.2 collective-permute-done.1.n1
  62.1 4.3 %collective-permute-done.4.s1 = bf16[4,32,768]{2,1,0:T(8,128)(2,1)} collective-permute-done((bf16[4,32,768]{2,1,0:T(8,128)(2,1)}, bf16[4,32,768]{2,1,0:T(8,128)(2,1)}, u32[]{:S(2)}, u32[]{:S(2)}) %collective-permute-start.4) | collective-permute-done | bytes 196640 | tf_op jit(solution)/shard_map/ppermute | solution.py:357
  67.1 1.3 turn_cotangent.1
  70.0 2.2 %all-to-all-done.1.refs_0_ = bf16[8,48,1536]{2,1,0:T(8,128)(2,1)S(1)} async-done(((bf16[8,48,1536]{2,1,0:T(8,128)(2,1)}), bf16[8,48,1536]{2,1,0:T(8,128)(2,1)S(1)}, u32[]{:S(2)}, u32[]{:S(2)}) %all-to-all-start.1) | async-done | bytes 1179680 | tf_op jit(solution)/shard_map/all_to_all | solution.py:373
  72.8 3.1 %collective-permute-done.8.cot_other = bf16[512,512]{1,0:T(8,128)(2,1)S(1)} collective-permute-done((bf16[512,512]{1,0:T(8,128)(2,1)S(1)}, bf16[512,512]{1,0:T(8,128)(2,1)S(1)}, u32[]{:S(2)}, u32[]{:S(2)}) %collective-permute-start.8) | collective-permute-done | bytes 524320 | tf_op jit(solution)/shard_map/ppermute | solution.py:352
  77.1 9.1 %layer.1 = (bf16[512,512]{1,0:T(8,128)(2,1)}, bf16[512,512]{1,0:T(8,128)(2,1)}, bf16[16,2,32,768]{3,2,1,0:T(8,128)(2,1)}) custom-call(s32[3]{0:T(128)} %copy-done.8, bf16[8,48,1024]{2,1,0:T(8,128)(2,1)} %copy-done.1, bf16[8,48,1024]{2,1,0:T(8,128)(2,1)} %collective-permute-done.other_ref.agg_other, bf16[8,48,1536]{2,1,0:T(8,128)(2,1)} %copy-done.2, ...), custom_call_target="tpu_custom_call" | custom-call | flops 3200000000 | bytes 9000000 | tf_op jit(solution)/shard_map/layer/pallas_call | solution.py:286
  86.3 7.5 %all-to-all-start.2 = ((bf16[32,32,768]{2,1,0:T(8,128)(2,1)}), bf16[32,32,768]{2,1,0:T(8,128)(2,1)S(1)}, u32[]{:S(2)}, u32[]{:S(2)}) async-start(bf16[32,32,768]{2,1,0:T(8,128)(2,1)} %bitcast.11), calls=%async_computation.2 | async-start | bytes 3145728 | tf_op jit(solution)/shard_map/all_to_all | solution.py:387
  94.1 1.6 %collective-permute-done.9.other_ref = bf16[512,512]{1,0:T(8,128)(2,1)S(1)} collective-permute-done((bf16[512,512]{1,0:T(8,128)(2,1)S(1)}, bf16[512,512]{1,0:T(8,128)(2,1)S(1)}, u32[]{:S(2)}, u32[]{:S(2)}) %collective-permute-start.9) | collective-permute-done | bytes 524320 | tf_op jit(solution)/shard_map/ppermute | solution.py:352
  95.8 3.2 %unturn_activation.1 = (bf16[512,1024]{1,0:T(8,128)(2,1)}, f32[8,128]{1,0:T(8,128)S(1)}) custom-call(s32[1]{0:T(128)} %bitcast.core_ref, bf16[512,512]{1,0:T(8,128)(2,1)S(1)} %copy-done.6, bf16[512,512]{1,0:T(8,128)(2,1)S(1)} %collective-permute-done.9.other_ref), custom_call_target="tpu_custom_call" | custom-call | bytes 4000000 | tf_op jit(solution)/shard_map/unturn_activation/pallas_call | solution.py:200
  98.9 18.8 %all-to-all-done.2.in_ref = bf16[32,32,768]{2,1,0:T(8,128)(2,1)S(1)} async-done(((bf16[32,32,768]{2,1,0:T(8,128)(2,1)}), bf16[32,32,768]{2,1,0:T(8,128)(2,1)S(1)}, u32[]{:S(2)}, u32[]{:S(2)}) %all-to-all-start.2) | async-done | bytes 1572896 | tf_op jit(solution)/shard_map/all_to_all | solution.py:387
  118.0 11.9 %all_to_all.20.in_ref = bf16[8,64,96]{2,1,0:T(8,128)(2,1)S(1)} all-to-all(bf16[8,64,96]{2,1,0:T(8,128)(2,1)S(1)} %add_pieces.1), channel_id=1, replica_groups=mesh['y'=4,'x'=4,'z'=8,'core'=2] {'z'}, dimensions={0} | all-to-all | bytes 196608 | tf_op jit(solution)/shard_map/all_to_all | solution.py:390
  (56 shorter events, 9.3 us)
Async XLA Ops:
  6.5 30.2 %all-to-all-start = ((bf16[8,48,1024]{2,1,0:T(8,128)(2,1)}), bf16[8,48,1024]{2,1,0:T(8,128)(2,1)S(1)}, u32[]{:S(2)}, u32[]{:S(2)}) async-start(bf16[8,48,1024]{2,1,0:T(8,128)(2,1)} %aggregate.2.rest_0_), calls=%async_computation | async-start | bytes 1572864 | tf_op jit(solution)/shard_map/all_to_all | solution.py:370
  15.1 5.6 %copy-start = (bf16[16384,48]{0,1:T(8,128)(2,1)S(1)}, bf16[16384,48]{0,1:T(8,128)(2,1)}, u32[]{:S(2)}) copy-start(bf16[16384,48]{0,1:T(8,128)(2,1)} %param.9) | copy-start | bytes 4718596
  15.1 5.6 %copy-start.7 = (s32[8192]{0:T(1024)S(1)}, s32[8192]{0:T(1024)}, u32[]{:S(2)}) copy-start(s32[8192]{0:T(1024)} %ids_ref.1) | copy-start | bytes 98308
  36.7 35.5 %all-to-all-start.1 = ((bf16[8,48,1536]{2,1,0:T(8,128)(2,1)}), bf16[8,48,1536]{2,1,0:T(8,128)(2,1)S(1)}, u32[]{:S(2)}, u32[]{:S(2)}) async-start(bf16[8,48,1536]{2,1,0:T(8,128)(2,1)} %own_rows.1.refs_1_), calls=%async_computation.1 | async-start | bytes 2359296 | tf_op jit(solution)/shard_map/all_to_all | solution.py:373
  42.0 18.4 %copy-start.13 = (f32[1024]{0:T(1024)S(1)}, f32[1024]{0:T(1024)}, u32[]{:S(2)}) copy-start(f32[1024]{0:T(1024)} %param.16) | copy-start | bytes 12292
  42.0 30.2 %copy-start.1 = (bf16[8,48,1024]{2,1,0:T(8,128)(2,1)}, bf16[8,48,1024]{2,1,0:T(8,128)(2,1)S(1)}, u32[]{:S(2)}) copy-start(bf16[8,48,1024]{2,1,0:T(8,128)(2,1)S(1)} %hand_on.2.mine_ref.agg_mine) | copy-start | bytes 2359300
  42.0 25.1 %copy-start.5 = (bf16[512,1024]{1,0:T(8,128)(2,1)S(1)}, bf16[512,1024]{1,0:T(8,128)(2,1)}, u32[]{:S(2)}) copy-start(bf16[512,1024]{1,0:T(8,128)(2,1)} %cot_ref.1) | copy-start | bytes 3145732
  42.0 2.5 %collective-permute-start = (bf16[8,48,1024]{2,1,0:T(8,128)(2,1)S(1)}, bf16[8,48,1024]{2,1,0:T(8,128)(2,1)}, u32[]{:S(2)}, u32[]{:S(2)}) collective-permute-start(bf16[8,48,1024]{2,1,0:T(8,128)(2,1)S(1)} %hand_on.2.mine_ref.agg_mine), channel_id=1, source_target_pairs={{0,1},{1,0},{2,3},{3,2},{4,5},{5,4},{6,7},{7,6},{8,9},{9,8},{10,11... | collective-permute-start | bytes 2359304 | tf_op jit(solution)/shard_map/ppermute | solution.py:352
  46.5 25.7 %copy-start.12 = (bf16[4,32,768]{2,1,0:T(8,128)(2,1)}, bf16[4,32,768]{2,1,0:T(8,128)(2,1)S(1)}, u32[]{:S(2)}) copy-start(bf16[4,32,768]{2,1,0:T(8,128)(2,1)S(1)} %get-tuple-element.14.n0) | copy-start | bytes 589828
  46.5 11.7 %collective-permute-start.3 = (bf16[4,32,768]{2,1,0:T(8,128)(2,1)S(1)}, bf16[4,32,768]{2,1,0:T(8,128)(2,1)S(1)}, u32[]{:S(2)}, u32[]{:S(2)}) collective-permute-start(bf16[4,32,768]{2,1,0:T(8,128)(2,1)S(1)} %get-tuple-element.14.n0), channel_id=1, source_target_pairs={{0,192},{64,0},{128,64},{192,128},{1,193},{65,1},{129,65},{193,129... | collective-permute-start | bytes 589832 | tf_op jit(solution)/shard_map/ppermute | solution.py:357
  49.5 11.3 %collective-permute-start.2 = (bf16[4,32,768]{2,1,0:T(8,128)(2,1)S(1)}, bf16[4,32,768]{2,1,0:T(8,128)(2,1)}, u32[]{:S(2)}, u32[]{:S(2)}) collective-permute-start(bf16[4,32,768]{2,1,0:T(8,128)(2,1)S(1)} %get-tuple-element.14.n0), channel_id=1, source_target_pairs={{0,128},{64,192},{128,0},{192,64},{1,129},{65,193},{129,1},{193,65... | collective-permute-start | bytes 589832 | tf_op jit(solution)/shard_map/ppermute | solution.py:357
  50.1 11.9 %collective-permute-start.1 = (bf16[4,32,768]{2,1,0:T(8,128)(2,1)S(1)}, bf16[4,32,768]{2,1,0:T(8,128)(2,1)}, u32[]{:S(2)}, u32[]{:S(2)}) collective-permute-start(bf16[4,32,768]{2,1,0:T(8,128)(2,1)S(1)} %get-tuple-element.14.n0), channel_id=1, source_target_pairs={{0,64},{64,128},{128,192},{192,0},{1,65},{65,129},{129,193},{193,1... | collective-permute-start | bytes 589832 | tf_op jit(solution)/shard_map/ppermute | solution.py:357
  51.1 11.0 %collective-permute-start.6 = (bf16[4,32,768]{2,1,0:T(8,128)(2,1)}, bf16[4,32,768]{2,1,0:T(8,128)(2,1)}, u32[]{:S(2)}, u32[]{:S(2)}) collective-permute-start(bf16[4,32,768]{2,1,0:T(8,128)(2,1)} %get-tuple-element.15.s0), channel_id=1, source_target_pairs={{0,48},{16,0},{32,16},{48,32},{1,49},{17,1},{33,17},{49,33},{2,50}... | collective-permute-start | bytes 589832 | tf_op jit(solution)/shard_map/ppermute | solution.py:357
  53.9 8.2 %collective-permute-start.5 = (bf16[4,32,768]{2,1,0:T(8,128)(2,1)}, bf16[4,32,768]{2,1,0:T(8,128)(2,1)}, u32[]{:S(2)}, u32[]{:S(2)}) collective-permute-start(bf16[4,32,768]{2,1,0:T(8,128)(2,1)} %get-tuple-element.15.s0), channel_id=1, source_target_pairs={{0,32},{16,48},{32,0},{48,16},{1,33},{17,49},{33,1},{49,17},{2,34}... | collective-permute-start | bytes 589832 | tf_op jit(solution)/shard_map/ppermute | solution.py:357
  58.9 7.5 %collective-permute-start.4 = (bf16[4,32,768]{2,1,0:T(8,128)(2,1)}, bf16[4,32,768]{2,1,0:T(8,128)(2,1)}, u32[]{:S(2)}, u32[]{:S(2)}) collective-permute-start(bf16[4,32,768]{2,1,0:T(8,128)(2,1)} %get-tuple-element.15.s0), channel_id=1, source_target_pairs={{0,16},{16,32},{32,48},{48,0},{1,17},{17,33},{33,49},{49,1},{2,18}... | collective-permute-start | bytes 589832 | tf_op jit(solution)/shard_map/ppermute | solution.py:357
  60.8 11.5 %copy-start.4 = (f32[512,1]{1,0:T(8,128)}, f32[512,1]{1,0:T(8,128)S(1)}, u32[]{:S(2)}) copy-start(f32[512,1]{1,0:T(8,128)S(1)} %reshape.28.refs_2_.bias_ref) | copy-start | bytes 6148
  60.8 11.4 %copy-start.8 = (s32[3]{0:T(128)}, s32[3]{0:T(128)S(1)}, u32[]{:S(2)}) copy-start(s32[3]{0:T(128)S(1)} %pad_add_fusion.refs_3_.place_ref) | copy-start | bytes 40
  72.2 3.7 %copy-start.2 = (bf16[8,48,1536]{2,1,0:T(8,128)(2,1)}, bf16[8,48,1536]{2,1,0:T(8,128)(2,1)S(1)}, u32[]{:S(2)}) copy-start(bf16[8,48,1536]{2,1,0:T(8,128)(2,1)S(1)} %hand_on.3.own_mine) | copy-start | bytes 3538948
  72.2 3.7 %collective-permute-start.7 = (bf16[8,48,1536]{2,1,0:T(8,128)(2,1)S(1)}, bf16[8,48,1536]{2,1,0:T(8,128)(2,1)S(1)}, u32[]{:S(2)}, u32[]{:S(2)}) collective-permute-start(bf16[8,48,1536]{2,1,0:T(8,128)(2,1)S(1)} %hand_on.3.own_mine), channel_id=1, source_target_pairs={{0,1},{1,0},{2,3},{3,2},{4,5},{5,4},{6,7},{7,6},{8,9},{9,8},{10,11... | collective-permute-start | bytes 3538952 | tf_op jit(solution)/shard_map/ppermute | solution.py:352
  72.3 3.6 %collective-permute-start.8 = (bf16[512,512]{1,0:T(8,128)(2,1)S(1)}, bf16[512,512]{1,0:T(8,128)(2,1)S(1)}, u32[]{:S(2)}, u32[]{:S(2)}) collective-permute-start(bf16[512,512]{1,0:T(8,128)(2,1)S(1)} %copy-done.10), channel_id=1, source_target_pairs={{0,1},{1,0},{2,3},{3,2},{4,5},{5,4},{6,7},{7,6},{8,9},{9,8},{10,11... | collective-permute-start | bytes 1572872 | tf_op jit(solution)/shard_map/ppermute | solution.py:352
  86.3 7.5 %copy-start.16 = (bf16[512,512]{1,0:T(8,128)(2,1)S(1)}, bf16[512,512]{1,0:T(8,128)(2,1)}, u32[]{:S(2)}) copy-start(bf16[512,512]{1,0:T(8,128)(2,1)} %get-tuple-element.19) | copy-start | bytes 1572868
  86.3 9.5 %copy-start.6 = (bf16[512,512]{1,0:T(8,128)(2,1)S(1)}, bf16[512,512]{1,0:T(8,128)(2,1)}, u32[]{:S(2)}) copy-start(bf16[512,512]{1,0:T(8,128)(2,1)} %get-tuple-element.18.mine_ref) | copy-start | bytes 1572868
  86.3 31.4 %all-to-all-start.2 = ((bf16[32,32,768]{2,1,0:T(8,128)(2,1)}), bf16[32,32,768]{2,1,0:T(8,128)(2,1)S(1)}, u32[]{:S(2)}, u32[]{:S(2)}) async-start(bf16[32,32,768]{2,1,0:T(8,128)(2,1)} %bitcast.11), calls=%async_computation.2 | async-start | bytes 3145728 | tf_op jit(solution)/shard_map/all_to_all | solution.py:387
  93.8 2.0 %collective-permute-start.9 = (bf16[512,512]{1,0:T(8,128)(2,1)S(1)}, bf16[512,512]{1,0:T(8,128)(2,1)S(1)}, u32[]{:S(2)}, u32[]{:S(2)}) collective-permute-start(bf16[512,512]{1,0:T(8,128)(2,1)S(1)} %copy-done.16), channel_id=1, source_target_pairs={{0,1},{1,0},{2,3},{3,2},{4,5},{5,4},{6,7},{7,6},{8,9},{9,8},{10,11... | collective-permute-start | bytes 1572872 | tf_op jit(solution)/shard_map/ppermute | solution.py:352
  (7 other events, 7.6 us)
